TPU v7x, 32 devices: a whole 2x2x4 slice. The times are simulated.
32 devices in a mesh: rep: 2 (over x), node: 2 (over core), local: 8 (over z, y).
Axes of the slice: x: 2, y: 2, z: 4, core: 2. Of those that a mesh axis runs over, the one named last changes fastest.
Arguments:
- attn_out: bfloat16 [64, 1024], P(('rep', 'node'), 'local'), parts along dimension 0, may hold values from -6 to 6
- o_proj: bfloat16 [1024, 7168], P('local'), may hold values from -0.1875 to 0.1875
- resid: bfloat16 [64, 7168], P(('rep', 'node', 'local')), parts along dimension 0, may hold values from -6 to 6
- norm_gain: float32 [7168], replicated, may hold values from 0.5 to 1.5
- routes: int32 [64, 8], P(('rep', 'node', 'local')), parts along dimension 0, may hold values from 0 to 15, all different within a row; in each aligned block of 2 rows (0 to 1, 2 to 3, ...) at most 2 rows name the same one
- route_w: bfloat16 [64, 8], P(('rep', 'node', 'local')), parts along dimension 0, may hold values from 0.19921875 to 1
- w_gate: bfloat16 [16, 7168, 2048], P(('node', 'local')), may hold values from -0.0625 to 0.0625
- w_up: bfloat16 [16, 7168, 2048], P(('node', 'local')), may hold values from -0.0625 to 0.0625
- w_down: bfloat16 [16, 2048, 7168], P(('node', 'local')), may hold values from -0.125 to 0.125
Outputs:
- layer_out: bfloat16 [64, 7168], P(('rep', 'node', 'local')), parts along dimension 0
There are 2 independent parts, one for each index of `rep`. A program takes and returns all parts, laid end to end along the dimension named above; an argument that names none is the same for every part. Nothing has to cross between parts.
Inputs may be any that keep to these rules, and one draw needn't show every extreme that they name: `routes`: each row names 8 different experts. Within the rows of one device (aligned blocks of 2 rows) no expert is named more than 2 times, and in some block some expert is named exactly 2 times.
All inputs are finite; a program needn't handle non-finite values.
Results may differ from a plain program's by a relative error of at most 0.0075.
Values may be sent and summed in bfloat16 or wider, within the bound.
No kernel may reach another device: no remote copies, remote signals or barrier semaphores. Data moves between devices by JAX's collectives and lax.ppermute only.
A program may use at most 128 MiB of HBM per device.

v0:
```python
import jax
import jax.numpy as jnp
from jax import lax
from jax.sharding import PartitionSpec as P

GROUP_EXPERTS = 8
MOST = 2


def plan_slots(expert_ids, pair_weights, expert_count, capacity, token_count):
    pair_count = expert_ids.shape[0]
    pairs_per_token = pair_count // token_count
    expert_hot = (expert_ids[:, None] == jnp.arange(expert_count, dtype=jnp.int32)[None, :]).astype(
        jnp.int32
    )
    earlier = jnp.cumsum(expert_hot, axis=0) - expert_hot
    slot_ids = jnp.sum(earlier * expert_hot, axis=1)
    usable = jnp.sum(expert_hot, axis=1) > 0
    position = expert_ids * capacity + slot_ids
    placed = (
        (position[:, None] == jnp.arange(expert_count * capacity, dtype=jnp.int32)[None, :])
        & usable[:, None]
    ).astype(jnp.float32)
    pair_token = jnp.arange(pair_count, dtype=jnp.int32) // pairs_per_token
    token_hot = (pair_token[:, None] == jnp.arange(token_count, dtype=jnp.int32)[None, :]).astype(
        jnp.float32
    )
    select = jnp.dot(
        placed.T, token_hot, precision=lax.Precision.HIGHEST, preferred_element_type=jnp.float32
    )
    combine = jnp.dot(
        token_hot.T,
        placed * pair_weights[:, None],
        precision=lax.Precision.HIGHEST,
        preferred_element_type=jnp.float32,
    )
    return (select, combine)


def run_expert(received, w_gate, w_up, w_down):
    senders, slot_count, model_width = received.shape
    flat_rows = received.reshape(senders * slot_count, model_width)
    gate_val = jnp.dot(flat_rows, w_gate[0], preferred_element_type=jnp.float32)
    up_val = jnp.dot(flat_rows, w_up[0], preferred_element_type=jnp.float32)
    activated = (jax.nn.silu(gate_val) * up_val).astype(jnp.bfloat16)
    pieces = jnp.dot(activated, w_down[0], preferred_element_type=jnp.float32).astype(jnp.bfloat16)
    return pieces.reshape(senders, slot_count, model_width)


def shards(attn_out, o_proj, resid, norm_gain, routes, route_w, w_gate, w_up, w_down):
    tok_rows = resid.shape[0]
    model_width = resid.shape[1]
    projected = lax.psum_scatter(
        jnp.dot(attn_out, o_proj, preferred_element_type=jnp.float32),
        "local",
        scatter_dimension=0,
        tiled=True,
    )
    hidden = resid.astype(jnp.float32) + projected
    mean_sq = jnp.mean(hidden * hidden, axis=-1, keepdims=True)
    normed = (hidden * lax.rsqrt(mean_sq + 1e-06) * norm_gain).astype(jnp.bfloat16)
    node_count = lax.axis_size("node")
    shard_count = lax.axis_size("local") // GROUP_EXPERTS
    summed = hidden
    expert_count = node_count * GROUP_EXPERTS
    select, combine = plan_slots(
        routes.reshape(-1), route_w.reshape(-1).astype(jnp.float32), expert_count, MOST, tok_rows
    )
    slot_rows = jnp.dot(
        select.astype(jnp.bfloat16), normed, preferred_element_type=jnp.float32
    ).astype(jnp.bfloat16)
    shaped = slot_rows.reshape(expert_count, 1, MOST, model_width)
    widened = jnp.broadcast_to(shaped, (expert_count, shard_count, MOST, model_width))
    returned = lax.all_to_all(
        run_expert(
            lax.all_to_all(
                widened.reshape(expert_count * shard_count, MOST, model_width),
                ("node", "local"),
                split_axis=0,
                concat_axis=0,
                tiled=True,
            ),
            w_gate,
            w_up,
            w_down,
        ),
        ("node", "local"),
        split_axis=0,
        concat_axis=0,
        tiled=True,
    )
    shaped = returned.reshape(expert_count, shard_count, MOST, model_width).astype(jnp.float32)
    expert_out = jnp.sum(shaped, axis=1).reshape(expert_count * MOST, model_width)
    slot_group = jnp.arange(expert_count * MOST, dtype=jnp.int32) // (MOST * GROUP_EXPERTS)
    for group_idx in range(node_count):
        masked = combine * (slot_group == group_idx).astype(jnp.float32)[None, :]
        group_out = jnp.dot(
            masked, expert_out, precision=lax.Precision.HIGHEST, preferred_element_type=jnp.float32
        ).astype(jnp.bfloat16)
        summed = summed + group_out.astype(jnp.float32)
    return summed.astype(jnp.bfloat16)


def solution(mesh):
    placed = (
        P(("rep", "node"), "local"),
        P("local", None),
        P(("rep", "node", "local"), None),
        P(),
        P(("rep", "node", "local"), None),
        P(("rep", "node", "local"), None),
        P(("node", "local"), None, None),
        P(("node", "local"), None, None),
        P(("node", "local"), None, None),
    )
    return jax.shard_map(
        shards,
        mesh=mesh,
        in_specs=placed,
        out_specs=P(("rep", "node", "local"), None),
        check_vma=False,
    )
```

profile of v0, /device:TPU:0, one launch (start us, length us, event | category | flops | bytes accessed | tf_op | source)
XLA Modules:
  0.0 167.5 jit_solution(16744512488504878344)
XLA Ops:
  6.5 0.0 copy-start
  6.5 0.0 all-reduce.3.cloned.1.call-start
  6.5 1.5 copy-done
  8.0 1.8 %fusion.50 = f32[16,7168]{1,0:T(8,128)} fusion(bf16[16,128]{1,0:T(8,128)(2,1)} %param.9, bf16[128,7168]{1,0:T(8,128)(2,1)S(1)} %copy-done), kind=kOutput, calls=%fused_computation.64 | convolution fusion | flops 29360128 | bytes 2297856 | tf_op jit(solution)/shard_map/dot_general | solution.py:54
  9.9 0.0 all-reduce.3.cloned.1.call-update
  9.9 0.8 reshape.78
  10.6 0.1 fusion.31
  10.8 0.2 fusion.35
  11.0 1.2 dynamic-slice
  12.9 0.3 convolution_convert_fusion.3
  13.1 72.3 %all-reduce.3.cloned.1.call-done = f32[16,7168]{1,0:T(8,128)} async-done(((f32[16,7168]{1,0:T(8,128)}), f32[16,7168]{1,0:T(8,128)}) %all-reduce.3.cloned.1.call-update) | async-done | bytes 458768
  85.5 1.1 multiply_reduce_fusion
  86.6 1.3 convolution_convert_fusion
  87.9 0.2 reshape_reshape.3
  88.1 18.4 %all_to_all.10 = bf16[16,2,7168]{2,1,0:T(2,128)(2,1)S(1)} all-to-all(bf16[16,2,7168]{2,1,0:T(2,128)(2,1)S(1)} %reshape_reshape.3), channel_id=1, replica_groups=mesh['rep'=2,'node'=2,'local'=8] {'node','local'}, dimensions={0} | all-to-all | bytes 917504 | tf_op jit(solution)/shard_map/all_to_all | solution.py:76
  106.4 0.2 reshape.79
  106.6 12.0 %fusion.4 = f32[32,2048]{1,0:T(8,128)S(1)} fusion(bf16[32,7168]{1,0:T(8,128)(2,1)S(1)} %reshape.79, bf16[1,7168,2048]{2,1,0:T(8,128)(2,1)} %param.15), kind=kOutput, calls=%fused_computation.4 | convolution fusion | flops 939524096 | bytes 30081024 | tf_op jit(solution)/shard_map/dot_general | solution.py:43
  118.6 0.0 copy-start.2
  118.6 0.0 copy-start.1
  118.6 20.8 %fusion.6 = bf16[32,7168]{1,0:T(8,128)(2,1)S(1)} fusion(bf16[1,2048,7168]{2,1,0:T(8,128)(2,1)} %param.17, bf16[32,7168]{1,0:T(8,128)(2,1)S(1)} %reshape.79, bf16[1,7168,2048]{2,1,0:T(8,128)(2,1)} %param.16, f32[32,2048]{1,0:T(8,128)S(1)} %fusion.4), kind=kOutput, calls=%fused_computation.6 | convolution fusion | flops 1879670784 | bytes 59899904 | tf_op jit(solution)/shard_map/dot_general | solution.py:46
  139.4 1.0 reshape.80
  140.4 3.6 %all-to-all-start.1 = ((bf16[16,2,7168]{2,1,0:T(2,128)(2,1)}), bf16[16,2,7168]{2,1,0:T(2,128)(2,1)S(1)}, u32[]{:S(2)}, u32[]{:S(2)}) async-start(bf16[16,2,7168]{2,1,0:T(2,128)(2,1)} %reshape.80), calls=%async_computation.1 | async-start | bytes 917504 | tf_op jit(solution)/shard_map/all_to_all | solution.py:74
  143.9 0.0 copy-done.2
  143.9 0.1 reshape.82
  144.0 0.3 fusion.29
  144.3 14.0 %all-to-all-done.1 = bf16[16,2,7168]{2,1,0:T(2,128)(2,1)S(1)} async-done(((bf16[16,2,7168]{2,1,0:T(2,128)(2,1)}), bf16[16,2,7168]{2,1,0:T(2,128)(2,1)S(1)}, u32[]{:S(2)}, u32[]{:S(2)}) %all-to-all-start.1) | async-done | bytes 458784 | tf_op jit(solution)/shard_map/all_to_all | solution.py:74
  158.3 0.2 reshape.81
  158.5 0.3 fusion.13
  158.8 0.0 copy-done.1
  158.8 1.9 %fusion.12 = bf16[2,7168]{1,0:T(2,128)(2,1)} fusion(f32[2,7168]{1,0:T(2,128)S(1)} %fusion.13, bf16[32,7168]{1,0:T(8,128)(2,1)S(1)} %reshape.81, f32[2,32]{1,0:T(2,128)S(1)} %fusion.29, f32[32]{0:T(128)S(1)} %compare_convert_fusion.1, f32[16,7168]{1,0:T(8,128)} %all-reduce.3.cloned.1.call-done, u32[]{:T(128)S(6)} %multiply.7, bf16[2,7168]{1,0:T(2,128)(2,1)S(1)} %copy-done.1), kind=kOutput, calls=%fused_computation.13 | convolution fusion | flops 5605440 | bytes 631172 | tf_op jit(solution)/shard_map/dot_general | solution.py:97
  (6 shorter events, 0.1 us)
Async XLA Ops:
  6.5 1.5 copy-start
  6.5 78.9 %all-reduce.3.cloned.1.call-start = ((), (), s32[]{:S(2)}) async-start(), calls=%async_computation.2 | async-start | bytes 917504
  118.6 25.4 %copy-start.2 = (bf16[2,8]{1,0:T(2,128)(2,1)S(1)}, bf16[2,8]{1,0:T(2,128)(2,1)}, u32[]{:S(2)}) copy-start(bf16[2,8]{1,0:T(2,128)(2,1)} %param.14) | copy-start | bytes 100
  118.6 40.2 %copy-start.1 = (bf16[2,7168]{1,0:T(2,128)(2,1)S(1)}, bf16[2,7168]{1,0:T(2,128)(2,1)}, u32[]{:S(2)}) copy-start(bf16[2,7168]{1,0:T(2,128)(2,1)} %param.11) | copy-start | bytes 86020
  140.4 17.9 %all-to-all-start.1 = ((bf16[16,2,7168]{2,1,0:T(2,128)(2,1)}), bf16[16,2,7168]{2,1,0:T(2,128)(2,1)S(1)}, u32[]{:S(2)}, u32[]{:S(2)}) async-start(bf16[16,2,7168]{2,1,0:T(2,128)(2,1)} %reshape.80), calls=%async_computation.1 | async-start | bytes 917504 | tf_op jit(solution)/shard_map/all_to_all | solution.py:74
Sparse Core Ops, SparseCore 0:
  10.8 74.6 all-reduce.2
where the time goes:
time: 168 us
  waiting for transfers between devices  86.4 us (51%)
  matrix products  38.6 us (23%)
  blocking collectives  18.4 us (11%)
  between operations  14.1 us (8%)
  local copies, waits for them, and re-layouts  5.07 us (3%)
  starting transfers between devices  3.56 us (2%)
    unnamed x2, waiting for transfers between devices  72.4 us
    dot_general x1, matrix products, run_expert(): jnp.dot(activated, w_down[0], preferred_element_type=jnp.float32)  20.8 us
    all_to_all x1, blocking collectives, shards(): lax.all_to_all(widened.reshape(expert_count * shard_count, MOST, model_wi...  18.4 us
    all_to_all x1, waiting for transfers between devices, shards(): lax.all_to_all(run_expert(lax.all_to_all(widened.reshape(expert_count * s...  14 us
    dot_general x1, matrix products, run_expert(): gate_val = jnp.dot(flat_rows, w_gate[0], preferred_element_type=jnp.float32)  12 us
    all_to_all x1, starting transfers between devices, shards(): lax.all_to_all(run_expert(lax.all_to_all(widened.reshape(expert_count * s...  3.56 us
  transfers between devices with their start and end apart: 2, of which 2 were waited for; matrix products, arithmetic and copies ran while one was open for 2% of the time, Pallas kernels for 0%

commit v1 on v0

v1 whole, which is shorter than its diff:
```python
import functools

import jax
import jax.numpy as jnp
from jax import lax
from jax.experimental import pallas as pl
from jax.experimental.pallas import tpu as pltpu
from jax.sharding import PartitionSpec as P

GROUP_EXPERTS = 8
LANES = 128
VMEM_OWN = 30 << 20
F32, BF16 = jnp.float32, jnp.bfloat16


def swap(x, axis, bit):
    return lax.ppermute(x, axis, [(i, i ^ bit) for i in range(lax.axis_size(axis))])


def fetch_kernel(first, rows, w_ref, after_ref, *refs):
    out_ref, sem = refs[-2:]
    part = pl.ds(first, rows)
    copy = pltpu.make_async_copy(w_ref.at[0, part], out_ref.at[part], sem)
    copy.start()
    copy.wait()


def fetch(weight, held, first, rows, after):
    _, depth, width = weight.shape
    anywhere = pl.BlockSpec(memory_space=pl.ANY)
    kept = [] if held is None else [pltpu.with_memory_space_constraint(held, pltpu.VMEM)]
    return pl.pallas_call(
        functools.partial(fetch_kernel, first, rows),
        out_shape=pltpu.VMEM((depth, width), BF16),
        in_specs=[anywhere, anywhere] + [pl.BlockSpec(memory_space=pltpu.VMEM)] * len(kept),
        out_specs=pl.BlockSpec(memory_space=pltpu.VMEM),
        scratch_shapes=[pltpu.SemaphoreType.DMA],
        input_output_aliases={2: 0} if kept else {},
        compiler_params=pltpu.CompilerParams(vmem_limit_bytes=VMEM_OWN),
        cost_estimate=pl.CostEstimate(flops=0, bytes_accessed=2 * rows * width, transcendentals=0),
    )(weight, after, *kept)


def expert_kernel(
    chunk_u, chunk_d, x_ref, mine_ref, gate_ref, up_hbm, down_hbm, keep_ref, send_ref,
    ring_u, ring_d, acc_g, acc_u, act_ref, sem_u, sem_d,
):
    rows = acc_g.shape[0]
    depth, width = gate_ref.shape
    slots_u, slots_d = ring_u.shape[0], ring_d.shape[0]
    steps_u, steps_d = depth // chunk_u, depth // chunk_d

    def copy_u(step):
        slot = step % slots_u
        return pltpu.make_async_copy(
            up_hbm.at[0, pl.ds(step * chunk_u, chunk_u)], ring_u.at[slot], sem_u.at[slot]
        )

    def copy_d(step):
        slot = step % slots_d
        return pltpu.make_async_copy(
            down_hbm.at[0, :, pl.ds(step * chunk_d, chunk_d)], ring_d.at[slot], sem_d.at[slot]
        )

    for step in range(min(slots_u, steps_u)):
        copy_u(step).start()
    for step in range(min(slots_d, steps_d)):
        copy_d(step).start()

    acc_g[...] = jnp.zeros_like(acc_g)
    acc_u[...] = jnp.zeros_like(acc_u)
    for step in range(steps_u):
        part = pl.ds(step * chunk_u, chunk_u)
        acc_g[...] += jnp.dot(x_ref[:, part], gate_ref[part, :], preferred_element_type=F32)
    for step in range(steps_u):
        part = pl.ds(step * chunk_u, chunk_u)
        copy_u(step).wait()
        acc_u[...] += jnp.dot(x_ref[:, part], ring_u[step % slots_u], preferred_element_type=F32)
        if step + slots_u < steps_u:
            copy_u(step + slots_u).start()
    gate_val = acc_g[...]
    act_ref[...] = (gate_val / (1.0 + jnp.exp(-gate_val)) * acc_u[...]).astype(BF16)
    coeff = jnp.sum(x_ref[:, pl.ds(depth, LANES)].astype(F32) * mine_ref[...], axis=1, keepdims=True)
    half = rows // 2
    for step in range(steps_d):
        part = pl.ds(step * chunk_d, chunk_d)
        copy_d(step).wait()
        piece = jnp.dot(act_ref[...], ring_d[step % slots_d], preferred_element_type=F32) * coeff
        keep_ref[:, part] = piece[:half]
        send_ref[:, part] = piece[half:].astype(BF16)
        if step + slots_d < steps_d:
            copy_d(step + slots_d).start()


def expert(x, mine, gate, w_up, w_down):
    rows = x.shape[0]
    depth, width = gate.shape
    chunk_u, chunk_d = depth // 7, depth // 7
    slots_u, slots_d = 3, 3
    vmem = pl.BlockSpec(memory_space=pltpu.VMEM)
    anywhere = pl.BlockSpec(memory_space=pl.ANY)
    return pl.pallas_call(
        functools.partial(expert_kernel, chunk_u, chunk_d),
        out_shape=(
            jax.ShapeDtypeStruct((rows // 2, depth), F32),
            jax.ShapeDtypeStruct((rows // 2, depth), BF16),
        ),
        in_specs=[vmem, vmem, vmem, anywhere, anywhere],
        out_specs=(vmem, vmem),
        scratch_shapes=[
            pltpu.VMEM((slots_u, chunk_u, width), BF16),
            pltpu.VMEM((slots_d, width, chunk_d), BF16),
            pltpu.VMEM((rows, width), F32),
            pltpu.VMEM((rows, width), F32),
            pltpu.VMEM((rows, width), BF16),
            pltpu.SemaphoreType.DMA((slots_u,)),
            pltpu.SemaphoreType.DMA((slots_d,)),
        ],
        compiler_params=pltpu.CompilerParams(vmem_limit_bytes=VMEM_OWN),
        cost_estimate=pl.CostEstimate(
            flops=6 * rows * depth * width, bytes_accessed=4 * depth * width, transcendentals=rows * width
        ),
    )(x, mine, pltpu.with_memory_space_constraint(gate, pltpu.VMEM), w_up, w_down)


def shards(attn_out, o_proj, resid, norm_gain, routes, route_w, w_gate, w_up, w_down):
    tok_rows, depth = resid.shape
    n_local, n_node = lax.axis_size("local"), lax.axis_size("node")
    expert_count = n_node * GROUP_EXPERTS
    shard_count = n_local // GROUP_EXPERTS
    here = lax.axis_index("local")
    mine = (lax.axis_index("node") * n_local + here) // shard_count
    bits = [1 << b for b in range(n_local.bit_length() - 1)]

    flip = [sum(bit for b, bit in enumerate(reversed(bits)) if j >> b & 1) for j in range(n_local)]
    owner = jnp.repeat(here ^ jnp.array(flip, jnp.int32), tok_rows) * tok_rows
    owner = owner + jnp.tile(jnp.arange(tok_rows, dtype=jnp.int32), n_local)
    order = (owner[:, None] == jnp.arange(n_local * tok_rows, dtype=jnp.int32)[None, :]).astype(BF16)

    hot = routes[:, :, None] == jnp.arange(LANES, dtype=jnp.int32)[None, None, :]
    picks = jnp.sum(jnp.where(hot, route_w.astype(F32)[:, :, None], 0.0), axis=1)
    mine_hot = (jnp.arange(LANES, dtype=jnp.int32) == mine).astype(F32)[None, :]
    order, picks, mine_hot = lax.optimization_barrier((order, picks, mine_hot))
    ordered = jnp.dot(order, attn_out, preferred_element_type=F32).astype(BF16)

    steps = len(bits) * 2
    unit = depth // 28
    cuts = [unit * (28 * s // steps) for s in range(steps + 1)]
    held = None

    def send(x, axis, bit, step):
        nonlocal held
        got = swap(x, axis, bit)
        held = fetch(w_gate, held, cuts[step], cuts[step + 1] - cuts[step], x)
        got, held = lax.optimization_barrier((got, held))
        return got

    w_gate, w_up, w_down = [pltpu.with_memory_space_constraint(w, pltpu.HBM) for w in (w_gate, w_up, w_down)]
    step = 0
    partial = jnp.dot(ordered, o_proj, preferred_element_type=F32)
    for bit in bits[:-1]:
        half = partial.shape[0] // 2
        partial = partial[:half] + send(partial[half:].astype(BF16), "local", bit, step).astype(F32)
        step += 1
    partial = jnp.concatenate([partial[:tok_rows] + resid.astype(F32), partial[tok_rows:]], axis=0)
    out = jnp.concatenate(
        [partial, jnp.concatenate([picks, jnp.zeros((tok_rows, LANES), F32)], axis=0)], axis=1
    ).astype(BF16)
    got = send(out, "local", bits[-1], step).astype(F32)
    step += 1
    got = jnp.concatenate([got[tok_rows:], got[:tok_rows]], axis=0)
    hidden = partial + got[:, :depth]
    columns = jnp.concatenate([picks, got[tok_rows:, depth:]], axis=0)
    mean_sq = jnp.mean(hidden * hidden, axis=-1, keepdims=True)
    normed = hidden * lax.rsqrt(mean_sq + 1e-06) * norm_gain
    tokens = jnp.concatenate([normed, columns], axis=1).astype(BF16)
    for bit in reversed(bits[:-1]):
        tokens = jnp.concatenate([tokens, send(tokens, "local", bit, step)], axis=0)
        step += 1
    tokens = jnp.concatenate([tokens, send(tokens, "node", 1, step)], axis=0)

    keep, away = expert(tokens, mine_hot, held, w_up, w_down)
    keep = keep + swap(away, "node", 1).astype(F32)
    for bit in bits:
        half = keep.shape[0] // 2
        keep = keep[:half] + swap(keep[half:].astype(BF16), "local", bit).astype(F32)
    return (hidden[:tok_rows] + keep).astype(BF16)


def solution(mesh):
    placed = (
        P(("rep", "node"), "local"),
        P("local", None),
        P(("rep", "node", "local"), None),
        P(),
        P(("rep", "node", "local"), None),
        P(("rep", "node", "local"), None),
        P(("node", "local"), None, None),
        P(("node", "local"), None, None),
        P(("node", "local"), None, None),
    )
    return jax.shard_map(
        shards,
        mesh=mesh,
        in_specs=placed,
        out_specs=P(("rep", "node", "local"), None),
        check_vma=False,
    )
```

time: 168 us -> 77.5 us (0.46)
  waiting for transfers between devices: 86.4 us -> 12.1 us
  Pallas kernels: 0 us -> 39.4 us
  matrix products: 38.6 us -> 1.14 us
  blocking collectives: 18.4 us -> 0 us
  between operations: 14.1 us -> 0.31 us
  starting transfers between devices: 3.56 us -> 17.1 us
  other arithmetic: 1.44 us -> 6.15 us
  local copies, waits for them, and re-layouts: 5.07 us -> 0.89 us
    unnamed x2 -> x0, waiting for transfers between devices: 72.4 us -> none
    pallas_call x0 -> x7, Pallas kernels: none -> 39.4 us  [the longest x1 25 us: expert(): pl.pallas_call(functools.partial(expert_kernel, chunk_u, chunk_d), out_sh...]
    dot_general x8 -> x1, matrix products: 38.6 us -> 1.14 us  [shards(): partial = jnp.dot(ordered, o_proj, preferred_element_type=F32)]
    all_to_all x1 -> x0, blocking collectives: 18.4 us -> none  [shards(): lax.all_to_all(widened.reshape(expert_count * shard_count, MOST, model_wi...]
    ppermute x0 -> x10, starting transfers between devices: none -> 17.1 us  [swap(): lax.ppermute(x, axis, [(i, i ^ bit) for i in range(lax.axis_size(axis))])]
    all_to_all x1 -> x0, waiting for transfers between devices: 14 us -> none  [shards(): lax.all_to_all(run_expert(lax.all_to_all(widened.reshape(expert_count * s...]
    ppermute x0 -> x10, waiting for transfers between devices: none -> 12.1 us  [swap(): lax.ppermute(x, axis, [(i, i ^ bit) for i in range(lax.axis_size(axis))])]
    all_to_all x1 -> x0, starting transfers between devices: 3.56 us -> none  [shards(): lax.all_to_all(run_expert(lax.all_to_all(widened.reshape(expert_count * s...]
  transfers between devices with their start and end apart: 2 -> 10, of which waited for: 2 -> 7; matrix products, arithmetic and copies ran while one was open for 2% -> 0% of each run, Pallas kernels for 0% -> 19%
where the time goes in v1:
time: 77.5 us; the launch traced here: 77.1 us
  Pallas kernels  39.4 us (51%)
  starting transfers between devices  17.1 us (22%)
  waiting for transfers between devices  12.1 us (16%)
  other arithmetic  6.15 us (8%)
  matrix products  1.14 us (1%)
  local copies, waits for them, and re-layouts  0.89 us (1%)
    pallas_call x1, Pallas kernels, expert(): pl.pallas_call(functools.partial(expert_kernel, chunk_u, chunk_d), out_sh...  25 us
    ppermute x10, starting transfers between devices, swap(): lax.ppermute(x, axis, [(i, i ^ bit) for i in range(lax.axis_size(axis))])  17.1 us
    pallas_call x6, Pallas kernels, fetch(): pl.pallas_call(functools.partial(fetch_kernel, first, rows), out_shape=pl...  14.4 us
    ppermute x10, waiting for transfers between devices, swap(): lax.ppermute(x, axis, [(i, i ^ bit) for i in range(lax.axis_size(axis))])  12.1 us
  transfers between devices with their start and end apart: 10, of which 7 were waited for; matrix products, arithmetic and copies ran while one was open for 0% of the time, Pallas kernels for 19%

profile of v1, /device:TPU:0, one launch (start us, length us, event | category | flops | bytes accessed | tf_op | source)
XLA Modules:
  0.0 77.1 jit_solution(16281277114096541408)
XLA Ops:
  0.0 0.5 compare_convert_fusion.mine_ref
  0.5 0.7 xor_multiply_fusion
  1.2 0.7 convert_element_type.54
  2.1 0.8 select_reduce_fusion
  2.9 1.1 %fusion = f32[16,7168]{1,0:T(8,128)S(1)} fusion(bf16[128,7168]{1,0:T(8,128)(2,1)S(1)} %copy-done, bf16[16,16]{1,0:T(8,128)(2,1)S(1)} %fusion.7, bf16[16,128]{1,0:T(8,128)(2,1)} %param.10), kind=kOutput, calls=%fused_computation.1 | convolution fusion | flops 29427712 | bytes 2298368 | tf_op jit(solution)/shard_map/dot_general | solution.py:160
  4.0 3.0 %collective-permute-start = (bf16[8,7168]{1,0:T(8,128)(2,1)S(1)}, bf16[8,7168]{1,0:T(8,128)(2,1)S(1)}, u32[]{:S(2)}, u32[]{:S(2)}) collective-permute-start(bf16[8,7168]{1,0:T(8,128)(2,1)S(1)} %slice.107.after_ref), channel_id=1, source_target_pairs={{0,1},{1,0},{2,3},{3,2},{4,5},{5,4},{6,7},{7,6},{8,9},{9,8},{10,11... | collective-permute-start | bytes 344072 | tf_op jit(solution)/shard_map/ppermute | solution.py:17
  7.1 2.2 %shard_map.100.refs_0_ = bf16[7168,2048]{1,0:T(8,128)(2,1)S(1)} custom-call(bf16[1,7168,2048]{2,1,0:T(8,128)(2,1)} %w_ref.11, bf16[8,7168]{1,0:T(8,128)(2,1)} %copy-done.4), custom_call_target="tpu_custom_call" | custom-call | bytes 4194304 | tf_op jit(solution)/shard_map/pallas_call | solution.py:32
  9.3 0.9 %collective-permute-done = bf16[8,7168]{1,0:T(8,128)(2,1)S(1)} collective-permute-done((bf16[8,7168]{1,0:T(8,128)(2,1)S(1)}, bf16[8,7168]{1,0:T(8,128)(2,1)S(1)}, u32[]{:S(2)}, u32[]{:S(2)}) %collective-permute-start) | collective-permute-done | bytes 114720 | tf_op jit(solution)/shard_map/ppermute | solution.py:17
  10.3 1.9 %collective-permute-start.1 = (bf16[4,7168]{1,0:T(4,128)(2,1)S(1)}, bf16[4,7168]{1,0:T(4,128)(2,1)S(1)}, u32[]{:S(2)}, u32[]{:S(2)}) collective-permute-start(bf16[4,7168]{1,0:T(4,128)(2,1)S(1)} %slice.109.after_ref), channel_id=1, source_target_pairs={{0,2},{1,3},{2,0},{3,1},{4,6},{5,7},{6,4},{7,5},{8,10},{9,11},{10,... | collective-permute-start | bytes 172040 | tf_op jit(solution)/shard_map/ppermute | solution.py:17
  12.2 2.5 %shard_map.101.refs_0_ = bf16[7168,2048]{1,0:T(8,128)(2,1)S(1)} custom-call(bf16[1,7168,2048]{2,1,0:T(8,128)(2,1)} %w_ref.11, bf16[4,7168]{1,0:T(4,128)(2,1)} %copy-done.7, bf16[7168,2048]{1,0:T(8,128)(2,1)S(1)} %shard_map.100.refs_0_), custom_call_target="tpu_custom_call", output_to_operand_aliasing={{}: (2, {})} | custom-call | bytes 5242880 | tf_op jit(solution)/shard_map/pallas_call | solution.py:32
  14.9 2.7 %collective-permute-start.2 = (bf16[4,7296]{1,0:T(4,128)(2,1)S(1)}, bf16[4,7296]{1,0:T(4,128)(2,1)S(1)}, u32[]{:S(2)}, u32[]{:S(2)}) collective-permute-start(bf16[4,7296]{1,0:T(4,128)(2,1)S(1)} %fusion.4.after_ref), channel_id=1, source_target_pairs={{0,4},{1,5},{2,6},{3,7},{4,0},{5,1},{6,2},{7,3},{8,12},{9,13},{10,... | collective-permute-start | bytes 175112 | tf_op jit(solution)/shard_map/ppermute | solution.py:17
  17.7 2.5 %shard_map.102.refs_0_ = bf16[7168,2048]{1,0:T(8,128)(2,1)S(1)} custom-call(bf16[1,7168,2048]{2,1,0:T(8,128)(2,1)} %w_ref.11, bf16[4,7296]{1,0:T(4,128)(2,1)} %copy-done.5, bf16[7168,2048]{1,0:T(8,128)(2,1)S(1)} %shard_map.101.refs_0_), custom_call_target="tpu_custom_call", output_to_operand_aliasing={{}: (2, {})} | custom-call | bytes 5242880 | tf_op jit(solution)/shard_map/pallas_call | solution.py:32
  20.2 0.2 multiply_reduce_fusion
  20.6 1.6 %collective-permute-start.3 = (bf16[4,7296]{1,0:T(4,128)(2,1)S(1)}, bf16[4,7296]{1,0:T(4,128)(2,1)S(1)}, u32[]{:S(2)}, u32[]{:S(2)}) collective-permute-start(bf16[4,7296]{1,0:T(4,128)(2,1)S(1)} %maximum_maximum_fusion.after_ref), channel_id=1, source_target_pairs={{0,2},{1,3},{2,0},{3,1},{4,6},{5,7},{6,4},{7,5},{8,10},{9,11},{10,... | collective-permute-start | bytes 175112 | tf_op jit(solution)/shard_map/ppermute | solution.py:17
  22.3 2.2 %shard_map.103.refs_0_ = bf16[7168,2048]{1,0:T(8,128)(2,1)S(1)} custom-call(bf16[1,7168,2048]{2,1,0:T(8,128)(2,1)} %w_ref.11, bf16[4,7296]{1,0:T(4,128)(2,1)} %copy-done.6, bf16[7168,2048]{1,0:T(8,128)(2,1)S(1)} %shard_map.102.refs_0_), custom_call_target="tpu_custom_call", output_to_operand_aliasing={{}: (2, {})} | custom-call | bytes 4194304 | tf_op jit(solution)/shard_map/pallas_call | solution.py:32
  24.5 0.4 collective-permute-done.3
  25.0 1.6 %collective-permute-start.4 = (bf16[8,7296]{1,0:T(8,128)(2,1)S(1)}, bf16[8,7296]{1,0:T(8,128)(2,1)S(1)}, u32[]{:S(2)}, u32[]{:S(2)}) collective-permute-start(bf16[8,7296]{1,0:T(8,128)(2,1)S(1)} %pad_maximum_fusion.2.after_ref), channel_id=1, source_target_pairs={{0,1},{1,0},{2,3},{3,2},{4,5},{5,4},{6,7},{7,6},{8,9},{9,8},{10,11... | collective-permute-start | bytes 350216 | tf_op jit(solution)/shard_map/ppermute | solution.py:17
  26.5 2.5 %shard_map.104.refs_0_ = bf16[7168,2048]{1,0:T(8,128)(2,1)S(1)} custom-call(bf16[1,7168,2048]{2,1,0:T(8,128)(2,1)} %w_ref.11, bf16[8,7296]{1,0:T(8,128)(2,1)} %copy-done.3, bf16[7168,2048]{1,0:T(8,128)(2,1)S(1)} %shard_map.103.refs_0_), custom_call_target="tpu_custom_call", output_to_operand_aliasing={{}: (2, {})} | custom-call | bytes 5242880 | tf_op jit(solution)/shard_map/pallas_call | solution.py:32
  29.0 0.8 %collective-permute-done.4 = bf16[8,7296]{1,0:T(8,128)(2,1)S(1)} collective-permute-done((bf16[8,7296]{1,0:T(8,128)(2,1)S(1)}, bf16[8,7296]{1,0:T(8,128)(2,1)S(1)}, u32[]{:S(2)}, u32[]{:S(2)}) %collective-permute-start.4) | collective-permute-done | bytes 116768 | tf_op jit(solution)/shard_map/ppermute | solution.py:17
  30.0 0.6 copy-done.2
  30.6 2.5 %shard_map.105.gate_ref = bf16[7168,2048]{1,0:T(8,128)(2,1)S(1)} custom-call(bf16[1,7168,2048]{2,1,0:T(8,128)(2,1)} %w_ref.11, bf16[16,7296]{1,0:T(8,128)(2,1)} %copy-done.2, bf16[7168,2048]{1,0:T(8,128)(2,1)S(1)} %shard_map.104.refs_0_), custom_call_target="tpu_custom_call", output_to_operand_aliasing={{}: (2, {})} | custom-call | bytes 5242880 | tf_op jit(solution)/shard_map/pallas_call | solution.py:32
  33.1 0.9 %pad_maximum_fusion.x_ref = bf16[32,7296]{1,0:T(8,128)(2,1)} fusion(bf16[16,7296]{1,0:T(8,128)(2,1)S(1)} %collective-permute-done.5, bf16[8,7296]{1,0:T(8,128)(2,1)S(1)} %collective-permute-done.4, bf16[4,7296]{1,0:T(4,128)(2,1)S(1)} %collective-permute-done.3, bf16[2,128]{1,0:T(2,128)(2,1)S(1)} %slice.68, bf16[2,128]{1,0:T(2,128)(2,1)S(1)} %select_reduce_fusion, ...), kind=kLoop, calls=%fused_computation.2 | loop fusion | flops 2801664 | bytes 933888 | tf_op jit(solution)/shard_map/concatenate | solution.py:180
  34.0 25.0 %shard_map.106 = (f32[16,7168]{1,0:T(8,128)}, bf16[16,7168]{1,0:T(8,128)(2,1)}) custom-call(bf16[32,7296]{1,0:T(8,128)(2,1)} %pad_maximum_fusion.x_ref, f32[1,128]{1,0:T(1,128)} %compare_convert_fusion.mine_ref, bf16[7168,2048]{1,0:T(8,128)(2,1)S(1)} %shard_map.105.gate_ref, bf16[1,7168,2048]{2,1,0:T(8,128)(2,1)} %up_hbm.1, bf16[1,2048,7168]{2,1,0:T(8,128)(2,1)} %down_hbm.1), custom_call_target="tpu_custom_call" | custom-call | flops 2818572288 | bytes 58720256 | tf_op jit(solution)/shard_map/pallas_call | solution.py:102
  59.2 1.7 %collective-permute-done.6 = bf16[16,7168]{1,0:T(8,128)(2,1)S(1)} collective-permute-done((bf16[16,7168]{1,0:T(8,128)(2,1)}, bf16[16,7168]{1,0:T(8,128)(2,1)S(1)}, u32[]{:S(2)}, u32[]{:S(2)}) %collective-permute-start.6) | collective-permute-done | bytes 229408 | tf_op jit(solution)/shard_map/ppermute | solution.py:17
  60.8 1.1 %convert_add_fusion = f32[16,7168]{1,0:T(8,128)S(1)} fusion(f32[16,7168]{1,0:T(8,128)} %get-tuple-element.37, bf16[16,7168]{1,0:T(8,128)(2,1)S(1)} %collective-permute-done.6), kind=kLoop, calls=%fused_computation.3 | loop fusion | flops 229376 | bytes 1146880 | tf_op jit(solution)/shard_map/add | solution.py:183
  61.9 1.6 %collective-permute-start.7 = (bf16[8,7168]{1,0:T(8,128)(2,1)S(1)}, bf16[8,7168]{1,0:T(8,128)(2,1)S(1)}, u32[]{:S(2)}, u32[]{:S(2)}) collective-permute-start(bf16[8,7168]{1,0:T(8,128)(2,1)S(1)} %slice.106), channel_id=1, source_target_pairs={{0,1},{1,0},{2,3},{3,2},{4,5},{5,4},{6,7},{7,6},{8,9},{9,8},{10,11... | collective-permute-start | bytes 344072 | tf_op jit(solution)/shard_map/ppermute | solution.py:17
  63.5 3.7 %collective-permute-done.7 = bf16[8,7168]{1,0:T(8,128)(2,1)S(1)} collective-permute-done((bf16[8,7168]{1,0:T(8,128)(2,1)S(1)}, bf16[8,7168]{1,0:T(8,128)(2,1)S(1)}, u32[]{:S(2)}, u32[]{:S(2)}) %collective-permute-start.7) | collective-permute-done | bytes 114720 | tf_op jit(solution)/shard_map/ppermute | solution.py:17
  67.2 1.6 %collective-permute-start.8 = (bf16[4,7168]{1,0:T(4,128)(2,1)S(1)}, bf16[4,7168]{1,0:T(4,128)(2,1)S(1)}, u32[]{:S(2)}, u32[]{:S(2)}) collective-permute-start(bf16[4,7168]{1,0:T(4,128)(2,1)S(1)} %slice.108), channel_id=1, source_target_pairs={{0,2},{1,3},{2,0},{3,1},{4,6},{5,7},{6,4},{7,5},{8,10},{9,11},{10,... | collective-permute-start | bytes 172040 | tf_op jit(solution)/shard_map/ppermute | solution.py:17
  68.9 2.6 %collective-permute-done.8 = bf16[4,7168]{1,0:T(4,128)(2,1)S(1)} collective-permute-done((bf16[4,7168]{1,0:T(4,128)(2,1)S(1)}, bf16[4,7168]{1,0:T(4,128)(2,1)S(1)}, u32[]{:S(2)}, u32[]{:S(2)}) %collective-permute-start.8) | collective-permute-done | bytes 57376 | tf_op jit(solution)/shard_map/ppermute | solution.py:17
  71.6 2.9 %collective-permute-start.9 = (bf16[2,7168]{1,0:T(2,128)(2,1)S(1)}, bf16[2,7168]{1,0:T(2,128)(2,1)S(1)}, u32[]{:S(2)}, u32[]{:S(2)}) collective-permute-start(bf16[2,7168]{1,0:T(2,128)(2,1)S(1)} %slice.110), channel_id=1, source_target_pairs={{0,4},{1,5},{2,6},{3,7},{4,0},{5,1},{6,2},{7,3},{8,12},{9,13},{10,... | collective-permute-start | bytes 86024 | tf_op jit(solution)/shard_map/ppermute | solution.py:17
  74.4 2.0 %collective-permute-done.9 = bf16[2,7168]{1,0:T(2,128)(2,1)S(1)} collective-permute-done((bf16[2,7168]{1,0:T(2,128)(2,1)S(1)}, bf16[2,7168]{1,0:T(2,128)(2,1)S(1)}, u32[]{:S(2)}, u32[]{:S(2)}) %collective-permute-start.9) | collective-permute-done | bytes 28704 | tf_op jit(solution)/shard_map/ppermute | solution.py:17
  76.4 0.7 fusion.6
  (46 shorter events, 1.1 us)
Async XLA Ops:
  0.0 2.9 %copy-start = (bf16[128,7168]{1,0:T(8,128)(2,1)S(1)}, bf16[128,7168]{1,0:T(8,128)(2,1)}, u32[]{:S(2)}) copy-start(bf16[128,7168]{1,0:T(8,128)(2,1)} %param.11) | copy-start | bytes 5505028
  4.0 3.0 %copy-start.4 = (bf16[8,7168]{1,0:T(8,128)(2,1)}, bf16[8,7168]{1,0:T(8,128)(2,1)S(1)}, u32[]{:S(2)}) copy-start(bf16[8,7168]{1,0:T(8,128)(2,1)S(1)} %slice.107.after_ref) | copy-start | bytes 344068
  4.0 6.2 %collective-permute-start = (bf16[8,7168]{1,0:T(8,128)(2,1)S(1)}, bf16[8,7168]{1,0:T(8,128)(2,1)S(1)}, u32[]{:S(2)}, u32[]{:S(2)}) collective-permute-start(bf16[8,7168]{1,0:T(8,128)(2,1)S(1)} %slice.107.after_ref), channel_id=1, source_target_pairs={{0,1},{1,0},{2,3},{3,2},{4,5},{5,4},{6,7},{7,6},{8,9},{9,8},{10,11... | collective-permute-start | bytes 344072 | tf_op jit(solution)/shard_map/ppermute | solution.py:17
  10.3 1.9 %copy-start.7 = (bf16[4,7168]{1,0:T(4,128)(2,1)}, bf16[4,7168]{1,0:T(4,128)(2,1)S(1)}, u32[]{:S(2)}) copy-start(bf16[4,7168]{1,0:T(4,128)(2,1)S(1)} %slice.109.after_ref) | copy-start | bytes 172036
  10.3 4.4 %copy-start.9 = (bf16[2,7168]{1,0:T(2,128)(2,1)S(1)}, bf16[2,7168]{1,0:T(2,128)(2,1)}, u32[]{:S(2)}) copy-start(bf16[2,7168]{1,0:T(2,128)(2,1)} %param.12) | copy-start | bytes 86020
  10.3 4.4 %collective-permute-start.1 = (bf16[4,7168]{1,0:T(4,128)(2,1)S(1)}, bf16[4,7168]{1,0:T(4,128)(2,1)S(1)}, u32[]{:S(2)}, u32[]{:S(2)}) collective-permute-start(bf16[4,7168]{1,0:T(4,128)(2,1)S(1)} %slice.109.after_ref), channel_id=1, source_target_pairs={{0,2},{1,3},{2,0},{3,1},{4,6},{5,7},{6,4},{7,5},{8,10},{9,11},{10,... | collective-permute-start | bytes 172040 | tf_op jit(solution)/shard_map/ppermute | solution.py:17
  14.9 2.8 %copy-start.5 = (bf16[4,7296]{1,0:T(4,128)(2,1)}, bf16[4,7296]{1,0:T(4,128)(2,1)S(1)}, u32[]{:S(2)}) copy-start(bf16[4,7296]{1,0:T(4,128)(2,1)S(1)} %fusion.4.after_ref) | copy-start | bytes 175108
  14.9 5.6 %copy-start.8 = (f32[7168]{0:T(1024)S(1)}, f32[7168]{0:T(1024)}, u32[]{:S(2)}) copy-start(f32[7168]{0:T(1024)} %param.13) | copy-start | bytes 86020
  14.9 5.2 %collective-permute-start.2 = (bf16[4,7296]{1,0:T(4,128)(2,1)S(1)}, bf16[4,7296]{1,0:T(4,128)(2,1)S(1)}, u32[]{:S(2)}, u32[]{:S(2)}) collective-permute-start(bf16[4,7296]{1,0:T(4,128)(2,1)S(1)} %fusion.4.after_ref), channel_id=1, source_target_pairs={{0,4},{1,5},{2,6},{3,7},{4,0},{5,1},{6,2},{7,3},{8,12},{9,13},{10,... | collective-permute-start | bytes 175112 | tf_op jit(solution)/shard_map/ppermute | solution.py:17
  20.6 1.7 %copy-start.6 = (bf16[4,7296]{1,0:T(4,128)(2,1)}, bf16[4,7296]{1,0:T(4,128)(2,1)S(1)}, u32[]{:S(2)}) copy-start(bf16[4,7296]{1,0:T(4,128)(2,1)S(1)} %maximum_maximum_fusion.after_ref) | copy-start | bytes 175108
  20.6 4.3 %collective-permute-start.3 = (bf16[4,7296]{1,0:T(4,128)(2,1)S(1)}, bf16[4,7296]{1,0:T(4,128)(2,1)S(1)}, u32[]{:S(2)}, u32[]{:S(2)}) collective-permute-start(bf16[4,7296]{1,0:T(4,128)(2,1)S(1)} %maximum_maximum_fusion.after_ref), channel_id=1, source_target_pairs={{0,2},{1,3},{2,0},{3,1},{4,6},{5,7},{6,4},{7,5},{8,10},{9,11},{10,... | collective-permute-start | bytes 175112 | tf_op jit(solution)/shard_map/ppermute | solution.py:17
  24.9 1.6 %copy-start.3 = (bf16[8,7296]{1,0:T(8,128)(2,1)}, bf16[8,7296]{1,0:T(8,128)(2,1)S(1)}, u32[]{:S(2)}) copy-start(bf16[8,7296]{1,0:T(8,128)(2,1)S(1)} %pad_maximum_fusion.2.after_ref) | copy-start | bytes 350212
  25.0 4.9 %collective-permute-start.4 = (bf16[8,7296]{1,0:T(8,128)(2,1)S(1)}, bf16[8,7296]{1,0:T(8,128)(2,1)S(1)}, u32[]{:S(2)}, u32[]{:S(2)}) collective-permute-start(bf16[8,7296]{1,0:T(8,128)(2,1)S(1)} %pad_maximum_fusion.2.after_ref), channel_id=1, source_target_pairs={{0,1},{1,0},{2,3},{3,2},{4,5},{5,4},{6,7},{7,6},{8,9},{9,8},{10,11... | collective-permute-start | bytes 350216 | tf_op jit(solution)/shard_map/ppermute | solution.py:17
  29.9 0.7 copy-start.2
  29.9 3.2 %collective-permute-start.5 = (bf16[16,7296]{1,0:T(8,128)(2,1)S(1)}, bf16[16,7296]{1,0:T(8,128)(2,1)S(1)}, u32[]{:S(2)}, u32[]{:S(2)}) collective-permute-start(bf16[16,7296]{1,0:T(8,128)(2,1)S(1)} %pad_maximum_fusion.1.after_ref), channel_id=1, source_target_pairs={{0,8},{8,0},{1,9},{9,1},{2,10},{10,2},{3,11},{11,3},{4,12},{12,4},... | collective-permute-start | bytes 700424 | tf_op jit(solution)/shard_map/ppermute | solution.py:17
  33.1 43.9 %copy-start.1 = (bf16[128,7168]{1,0:T(8,128)(2,1)S(1)}, bf16[128,7168]{1,0:T(8,128)(2,1)}, u32[]{:S(2)}) copy-start(bf16[128,7168]{1,0:T(8,128)(2,1)} %param.11) | copy-start | bytes 5505028
  59.1 1.8 %collective-permute-start.6 = (bf16[16,7168]{1,0:T(8,128)(2,1)}, bf16[16,7168]{1,0:T(8,128)(2,1)S(1)}, u32[]{:S(2)}, u32[]{:S(2)}) collective-permute-start(bf16[16,7168]{1,0:T(8,128)(2,1)} %get-tuple-element.38), channel_id=1, source_target_pairs={{0,8},{8,0},{1,9},{9,1},{2,10},{10,2},{3,11},{11,3},{4,12},{12,4},... | collective-permute-start | bytes 688136 | tf_op jit(solution)/shard_map/ppermute | solution.py:17
  61.9 5.3 %collective-permute-start.7 = (bf16[8,7168]{1,0:T(8,128)(2,1)S(1)}, bf16[8,7168]{1,0:T(8,128)(2,1)S(1)}, u32[]{:S(2)}, u32[]{:S(2)}) collective-permute-start(bf16[8,7168]{1,0:T(8,128)(2,1)S(1)} %slice.106), channel_id=1, source_target_pairs={{0,1},{1,0},{2,3},{3,2},{4,5},{5,4},{6,7},{7,6},{8,9},{9,8},{10,11... | collective-permute-start | bytes 344072 | tf_op jit(solution)/shard_map/ppermute | solution.py:17
  67.2 4.2 %collective-permute-start.8 = (bf16[4,7168]{1,0:T(4,128)(2,1)S(1)}, bf16[4,7168]{1,0:T(4,128)(2,1)S(1)}, u32[]{:S(2)}, u32[]{:S(2)}) collective-permute-start(bf16[4,7168]{1,0:T(4,128)(2,1)S(1)} %slice.108), channel_id=1, source_target_pairs={{0,2},{1,3},{2,0},{3,1},{4,6},{5,7},{6,4},{7,5},{8,10},{9,11},{10,... | collective-permute-start | bytes 172040 | tf_op jit(solution)/shard_map/ppermute | solution.py:17
  71.6 4.8 %collective-permute-start.9 = (bf16[2,7168]{1,0:T(2,128)(2,1)S(1)}, bf16[2,7168]{1,0:T(2,128)(2,1)S(1)}, u32[]{:S(2)}, u32[]{:S(2)}) collective-permute-start(bf16[2,7168]{1,0:T(2,128)(2,1)S(1)} %slice.110), channel_id=1, source_target_pairs={{0,4},{1,5},{2,6},{3,7},{4,0},{5,1},{6,2},{7,3},{8,12},{9,13},{10,... | collective-permute-start | bytes 86024 | tf_op jit(solution)/shard_map/ppermute | solution.py:17

commit v2 on v1

v2 whole, which is shorter than its diff:
```python
import functools

import jax
import jax.numpy as jnp
from jax import lax
from jax.experimental import pallas as pl
from jax.experimental.pallas import tpu as pltpu
from jax.sharding import PartitionSpec as P

GROUP_EXPERTS = 8
LANES = 128
VMEM_OWN = 26 << 20
SLOTS = 4
HAVE = 1
F32, BF16 = jnp.float32, jnp.bfloat16
VMEM = pl.BlockSpec(memory_space=pltpu.VMEM)
ANYWHERE = pl.BlockSpec(memory_space=pl.ANY)


def swap(x, axis, bit):
    return lax.ppermute(x, axis, [(i, i ^ bit) for i in range(lax.axis_size(axis))])


def in_vmem(x):
    return pltpu.with_memory_space_constraint(x, pltpu.VMEM)


def project_kernel(n_local, tok_rows, attn_ref, proj_ref, keep_ref, send_ref):
    count = n_local * tok_rows
    here = lax.axis_index("local")
    place = lax.broadcasted_iota(jnp.int32, (count, count), 0)
    block, flip = place // tok_rows, 0
    bits = n_local.bit_length() - 1
    for b in range(bits):
        flip = flip | (((block >> b) & 1) << (bits - 1 - b))
    owner = (here ^ flip) * tok_rows + place % tok_rows
    order = (owner == lax.broadcasted_iota(jnp.int32, (count, count), 1)).astype(BF16)
    ordered = jnp.dot(order, attn_ref[...], preferred_element_type=F32).astype(BF16)
    half = count // 2
    partial = jnp.dot(ordered, proj_ref[...], preferred_element_type=F32)
    keep_ref[...] = partial[:half]
    send_ref[...] = partial[half:].astype(BF16)


def project(attn_out, o_proj, tok_rows):
    depth = o_proj.shape[1]
    half = attn_out.shape[0] // 2
    return pl.pallas_call(
        functools.partial(project_kernel, lax.axis_size("local"), tok_rows),
        out_shape=(pltpu.VMEM((half, depth), F32), pltpu.VMEM((half, depth), BF16)),
        in_specs=[VMEM, VMEM],
        out_specs=(VMEM, VMEM),
        compiler_params=pltpu.CompilerParams(vmem_limit_bytes=VMEM_OWN),
    )(attn_out, o_proj)


def fetch_kernel(depth, first, last, gate_hbm, up_hbm, after_ref, *refs):
    held_ref, sem = refs[-2:]
    copies = []
    if first < depth:
        part = pl.ds(first, min(last, depth) - first)
        copies.append(pltpu.make_async_copy(gate_hbm.at[0, part], held_ref.at[part], sem.at[0]))
    if last > depth:
        first = max(first, depth)
        source = up_hbm.at[0, pl.ds(first - depth, last - first)]
        copies.append(pltpu.make_async_copy(source, held_ref.at[pl.ds(first, last - first)], sem.at[1]))
    for copy in copies:
        copy.start()
    for copy in copies:
        copy.wait()


def fetch(w_gate, w_up, held, total, first, last, after):
    _, depth, width = w_gate.shape
    kept = [] if held is None else [in_vmem(held)]
    return pl.pallas_call(
        functools.partial(fetch_kernel, depth, first, last),
        out_shape=pltpu.VMEM((total, width), BF16),
        in_specs=[ANYWHERE] * 3 + [VMEM] * len(kept),
        out_specs=VMEM,
        scratch_shapes=[pltpu.SemaphoreType.DMA((2,))],
        input_output_aliases={3: 0} if kept else {},
        compiler_params=pltpu.CompilerParams(vmem_limit_bytes=VMEM_OWN),
        cost_estimate=pl.CostEstimate(flops=0, bytes_accessed=2 * (last - first) * width, transcendentals=0),
    )(w_gate, w_up, after, *kept)


def picks_kernel(routes_ref, route_w_ref, after_ref, picks_ref):
    tok_rows, top = routes_ref.shape
    lane = lax.broadcasted_iota(jnp.int32, (tok_rows, LANES), 1)
    total = jnp.zeros((tok_rows, LANES), F32)
    weights = route_w_ref[...].astype(F32)
    for k in range(top):
        total = total + jnp.where(routes_ref[:, k : k + 1] == lane, weights[:, k : k + 1], 0.0)
    picks_ref[...] = total


def picks_of(routes, route_w, after):
    return pl.pallas_call(
        picks_kernel,
        out_shape=pltpu.VMEM((routes.shape[0], LANES), F32),
        in_specs=[VMEM, VMEM, ANYWHERE],
        out_specs=VMEM,
        compiler_params=pltpu.CompilerParams(vmem_limit_bytes=VMEM_OWN),
    )(routes, route_w, after)


def expert_kernel(
    n_local, chunk, own_ref, other_ref, held_ref, up_hbm, down_hbm, keep_ref, send_ref,
    ring, x_ref, acc_g, acc_u, act_ref, sem,
):
    half = own_ref.shape[0]
    _, depth, width = up_hbm.shape
    slots, parts = ring.shape[0], width // chunk
    have = held_ref.shape[0] - depth
    steps = [(True, at) for at in range(have, depth, chunk)] + [(False, at) for at in range(0, depth, chunk)]

    def copies(step):
        is_up, at = steps[step]
        slot = step % slots
        for p in range(parts):
            cut = pl.ds(p * chunk, chunk)
            source = up_hbm.at[0, pl.ds(at, chunk), cut] if is_up else down_hbm.at[0, cut, pl.ds(at, chunk)]
            yield pltpu.make_async_copy(source, ring.at[slot, cut], sem.at[slot, p])

    def start(step):
        for copy in copies(step):
            copy.start()

    for step in range(min(slots, len(steps))):
        start(step)
    x_ref[:half] = own_ref[:, :depth]
    x_ref[half:] = other_ref[:, :depth]
    shard_count = n_local // GROUP_EXPERTS
    mine = (lax.axis_index("node") * n_local + lax.axis_index("local")) // shard_count
    mine_hot = lax.broadcasted_iota(jnp.int32, (1, LANES), 1) == mine
    coeff = jnp.concatenate(
        [
            jnp.sum(jnp.where(mine_hot, ref[:, depth:].astype(F32), 0.0), axis=1, keepdims=True)
            for ref in (own_ref, other_ref)
        ],
        axis=0,
    )

    def add(acc, w_ref, row, column):
        rows, columns = w_ref.shape
        part = pl.ds(column, columns)
        product = jnp.dot(x_ref[:, row : row + rows], w_ref[...], preferred_element_type=F32)
        acc[:, part] = product if row == 0 else acc[:, part] + product

    for row in range(0, depth, chunk):
        add(acc_g, held_ref.at[pl.ds(row, chunk)], row, 0)
    for row in range(0, have, chunk):
        add(acc_u, held_ref.at[pl.ds(depth + row, chunk)], row, 0)
    for step, (is_up, at) in enumerate(steps):
        slot = step % slots
        for copy in copies(step):
            copy.wait()
        if is_up:
            for p in range(parts):
                add(acc_u, ring.at[slot, pl.ds(p * chunk, chunk)], at, p * chunk)
        else:
            if at == 0:
                gate_val = acc_g[...]
                act_ref[...] = (gate_val / (1.0 + jnp.exp(-gate_val)) * acc_u[...]).astype(BF16)
            piece = jnp.dot(act_ref[...], ring[slot], preferred_element_type=F32) * coeff
            keep_ref[:, pl.ds(at, chunk)] = piece[:half]
            send_ref[:, pl.ds(at, chunk)] = piece[half:].astype(BF16)
        if step + slots < len(steps):
            start(step + slots)


def expert(own, other, held, w_up, w_down, chunk):
    half = own.shape[0]
    rows = 2 * half
    _, depth, width = w_up.shape
    slots = SLOTS
    return pl.pallas_call(
        functools.partial(expert_kernel, lax.axis_size("local"), chunk),
        out_shape=(jax.ShapeDtypeStruct((half, depth), F32), jax.ShapeDtypeStruct((half, depth), BF16)),
        in_specs=[VMEM, VMEM, VMEM, ANYWHERE, ANYWHERE],
        out_specs=(VMEM, VMEM),
        scratch_shapes=[
            pltpu.VMEM((slots, width, chunk), BF16),
            pltpu.VMEM((rows, depth), BF16),
            pltpu.VMEM((rows, width), F32),
            pltpu.VMEM((rows, width), F32),
            pltpu.VMEM((rows, width), BF16),
            pltpu.SemaphoreType.DMA((slots, width // chunk)),
        ],
        compiler_params=pltpu.CompilerParams(vmem_limit_bytes=VMEM_OWN),
        cost_estimate=pl.CostEstimate(
            flops=6 * rows * depth * width, bytes_accessed=4 * depth * width, transcendentals=rows * width
        ),
    )(own, other, in_vmem(held), w_up, w_down)


def shards(attn_out, o_proj, resid, norm_gain, routes, route_w, w_gate, w_up, w_down):
    tok_rows, depth = resid.shape
    width = w_gate.shape[2]
    n_local = lax.axis_size("local")
    bits = [1 << b for b in range(n_local.bit_length() - 1)]
    w_gate, w_up, w_down = [pltpu.with_memory_space_constraint(w, pltpu.HBM) for w in (w_gate, w_up, w_down)]

    chunk = min(1024, width)
    total = depth + HAVE * chunk
    shares = [1] + [3] + [2] * (2 * len(bits) - 3) + [3, 1]
    unit = depth // 28
    cuts = [total // unit * sum(shares[:s]) // sum(shares) * unit for s in range(len(shares) + 1)]
    held, step = fetch(w_gate, w_up, None, total, 0, cuts[1], attn_out), 1
    attn_out, held = lax.optimization_barrier((attn_out, held))

    def send(x, axis, bit, more=()):
        nonlocal held, step
        got = swap(x, axis, bit)
        held = fetch(w_gate, w_up, held, total, cuts[step], cuts[step + 1], x)
        got, held, *more = lax.optimization_barrier((got, held, *more))
        step += 1
        return (got, *more) if more else got

    keep, away = project(attn_out, o_proj, tok_rows)
    got, picks = send(away, "local", bits[0], (picks_of(routes, route_w, away),))
    partial = keep + got.astype(F32)
    for bit in bits[1:-1]:
        half = partial.shape[0] // 2
        partial = partial[:half] + send(partial[half:].astype(BF16), "local", bit).astype(F32)
    partial = jnp.concatenate([partial[:tok_rows] + resid.astype(F32), partial[tok_rows:]], axis=0)
    out = jnp.concatenate(
        [partial, jnp.concatenate([picks, jnp.zeros((tok_rows, LANES), F32)], axis=0)], axis=1
    ).astype(BF16)
    got = send(out, "local", bits[-1]).astype(F32)
    got = jnp.concatenate([got[tok_rows:], got[:tok_rows]], axis=0)
    hidden = partial + got[:, :depth]
    columns = jnp.concatenate([picks, got[tok_rows:, depth:]], axis=0)
    mean_sq = jnp.mean(hidden * hidden, axis=-1, keepdims=True)
    normed = hidden * lax.rsqrt(mean_sq + 1e-06) * norm_gain
    tokens = jnp.concatenate([normed, columns], axis=1).astype(BF16)
    for bit in reversed(bits[:-1]):
        tokens = jnp.concatenate([tokens, send(tokens, "local", bit)], axis=0)
    other = send(tokens, "node", 1)

    keep, away = expert(tokens, other, held, w_up, w_down, chunk)
    keep = keep + swap(away, "node", 1).astype(F32)
    for bit in bits:
        half = keep.shape[0] // 2
        keep = keep[:half] + swap(keep[half:].astype(BF16), "local", bit).astype(F32)
    return (hidden[:tok_rows] + keep).astype(BF16)


def solution(mesh):
    placed = (
        P(("rep", "node"), "local"),
        P("local", None),
        P(("rep", "node", "local"), None),
        P(),
        P(("rep", "node", "local"), None),
        P(("rep", "node", "local"), None),
        P(("node", "local"), None, None),
        P(("node", "local"), None, None),
        P(("node", "local"), None, None),
    )
    return jax.shard_map(
        shards,
        mesh=mesh,
        in_specs=placed,
        out_specs=P(("rep", "node", "local"), None),
        check_vma=False,
    )
```

time: 77.5 us -> 72.4 us (0.934)
  other arithmetic: 6.15 us -> 2.5 us
  starting transfers between devices: 17.1 us -> 15.1 us
  local copies, waits for them, and re-layouts: 0.89 us -> 2.75 us
  matrix products: 1.14 us -> 0 us
    ppermute x10, starting transfers between devices: 17.1 us -> 15.1 us  [swap(): lax.ppermute(x, axis, [(i, i ^ bit) for i in range(lax.axis_size(axis))])]
    unnamed x20 -> x28, local copies, waits for them, and re-layouts: 0.65 us -> 2.6 us
    convert_element_type x3 -> x0, other arithmetic: 1.25 us -> none  [the longest x1 0.66 us: shards(): route_w.astype(F32)[:, :, None]]
    dot_general x1 -> x0, matrix products: 1.14 us -> none  [shards(): partial = jnp.dot(ordered, o_proj, preferred_element_type=F32)]
    concatenate x3 -> x2, other arithmetic: 1.04 us -> 0.16 us  [shards(): tokens = jnp.concatenate([tokens, send(tokens, 'local', bit)], axis=0)]
    pallas_call x7 -> x10, Pallas kernels: 39.4 us -> 38.7 us  [the longest x1 21.4 us: expert(): pl.pallas_call(functools.partial(expert_kernel, lax.axis_size('local'), c...]
  transfers between devices with their start and end apart: 10 -> 10, of which waited for: 7 -> 7; matrix products, arithmetic and copies ran while one was open for 0% -> 0% of each run, Pallas kernels for 19% -> 21%
where the time goes in v2:
time: 72.4 us; the launch traced here: 72 us
  Pallas kernels  38.7 us (53%)
  starting transfers between devices  15.1 us (21%)
  waiting for transfers between devices  12.6 us (17%)
  local copies, waits for them, and re-layouts  2.75 us (4%)
  other arithmetic  2.5 us (3%)
    pallas_call x1, Pallas kernels, expert(): pl.pallas_call(functools.partial(expert_kernel, lax.axis_size('local'), c...  21.4 us
    pallas_call x7, Pallas kernels, fetch(): pl.pallas_call(functools.partial(fetch_kernel, depth, first, last), out_s...  16.7 us
    ppermute x10, starting transfers between devices, swap(): lax.ppermute(x, axis, [(i, i ^ bit) for i in range(lax.axis_size(axis))])  15.1 us
    ppermute x10, waiting for transfers between devices, swap(): lax.ppermute(x, axis, [(i, i ^ bit) for i in range(lax.axis_size(axis))])  12.6 us
    unnamed x28, local copies, waits for them, and re-layouts  2.6 us
  transfers between devices with their start and end apart: 10, of which 7 were waited for; matrix products, arithmetic and copies ran while one was open for 0% of the time, Pallas kernels for 21%

profile of v2, /device:TPU:0, one launch (start us, length us, event | category | flops | bytes accessed | tf_op | source)
XLA Modules:
  0.0 72.0 jit_solution(667067911503559214)
XLA Ops:
  0.0 1.7 %shard_map.91.refs_0_ = bf16[8192,2048]{1,0:T(8,128)(2,1)S(1)} custom-call(bf16[1,7168,2048]{2,1,0:T(8,128)(2,1)} %gate_hbm.13, bf16[1,7168,2048]{2,1,0:T(8,128)(2,1)} %up_hbm.15, bf16[16,128]{1,0:T(8,128)(2,1)} %attn_ref), custom_call_target="tpu_custom_call" | custom-call | bytes 2097152 | tf_op jit(solution)/shard_map/pallas_call | solution.py:76
  1.8 0.4 copy-done
  2.1 0.5 shard_map.92
  2.6 3.0 %collective-permute-start = (bf16[8,7168]{1,0:T(8,128)(2,1)S(1)}, bf16[8,7168]{1,0:T(8,128)(2,1)S(1)}, u32[]{:S(2)}, u32[]{:S(2)}) collective-permute-start(bf16[8,7168]{1,0:T(8,128)(2,1)S(1)} %get-tuple-element.26.after_ref), channel_id=1, source_target_pairs={{0,1},{1,0},{2,3},{3,2},{4,5},{5,4},{6,7},{7,6},{8,9},{9,8},{10,11... | collective-permute-start | bytes 344072 | tf_op jit(solution)/shard_map/ppermute | solution.py:21
  5.7 3.1 %shard_map.93.refs_0_ = bf16[8192,2048]{1,0:T(8,128)(2,1)S(1)} custom-call(bf16[1,7168,2048]{2,1,0:T(8,128)(2,1)} %gate_hbm.13, bf16[1,7168,2048]{2,1,0:T(8,128)(2,1)} %up_hbm.15, bf16[8,7168]{1,0:T(8,128)(2,1)} %copy-done.1, bf16[8192,2048]{1,0:T(8,128)(2,1)S(1)} %shard_map.91.refs_0_), custom_call_target="tpu_custom_call", output_to_operand_aliasing={{}: (3, {})} | custom-call | bytes 7340032 | tf_op jit(solution)/shard_map/pallas_call | solution.py:76
  8.8 0.9 %copy-done.2 = bf16[8,7168]{1,0:T(8,128)(2,1)S(1)} copy-done((bf16[8,7168]{1,0:T(8,128)(2,1)S(1)}, bf16[8,7168]{1,0:T(8,128)(2,1)}, u32[]{:S(2)}) %copy-start.2) | copy-done | bytes 114712
  9.9 1.6 %collective-permute-start.1 = (bf16[4,7168]{1,0:T(4,128)(2,1)S(1)}, bf16[4,7168]{1,0:T(4,128)(2,1)S(1)}, u32[]{:S(2)}, u32[]{:S(2)}) collective-permute-start(bf16[4,7168]{1,0:T(4,128)(2,1)S(1)} %slice.95.after_ref), channel_id=1, source_target_pairs={{0,2},{1,3},{2,0},{3,1},{4,6},{5,7},{6,4},{7,5},{8,10},{9,11},{10,... | collective-permute-start | bytes 172040 | tf_op jit(solution)/shard_map/ppermute | solution.py:21
  11.5 2.2 %shard_map.95.refs_0_ = bf16[8192,2048]{1,0:T(8,128)(2,1)S(1)} custom-call(bf16[1,7168,2048]{2,1,0:T(8,128)(2,1)} %gate_hbm.13, bf16[1,7168,2048]{2,1,0:T(8,128)(2,1)} %up_hbm.15, bf16[4,7168]{1,0:T(4,128)(2,1)} %copy-done.11, bf16[8192,2048]{1,0:T(8,128)(2,1)S(1)} %shard_map.93.refs_0_), custom_call_target="tpu_custom_call", output_to_operand_aliasing={{}: (3, {})} | custom-call | bytes 4194304 | tf_op jit(solution)/shard_map/pallas_call | solution.py:76
  13.7 0.4 collective-permute-done.1
  14.3 2.7 %collective-permute-start.2 = (bf16[4,7296]{1,0:T(4,128)(2,1)S(1)}, bf16[4,7296]{1,0:T(4,128)(2,1)S(1)}, u32[]{:S(2)}, u32[]{:S(2)}) collective-permute-start(bf16[4,7296]{1,0:T(4,128)(2,1)S(1)} %fusion.3.after_ref), channel_id=1, source_target_pairs={{0,4},{1,5},{2,6},{3,7},{4,0},{5,1},{6,2},{7,3},{8,12},{9,13},{10,... | collective-permute-start | bytes 175112 | tf_op jit(solution)/shard_map/ppermute | solution.py:21
  17.0 2.5 %shard_map.96.refs_0_ = bf16[8192,2048]{1,0:T(8,128)(2,1)S(1)} custom-call(bf16[1,7168,2048]{2,1,0:T(8,128)(2,1)} %gate_hbm.13, bf16[1,7168,2048]{2,1,0:T(8,128)(2,1)} %up_hbm.15, bf16[4,7296]{1,0:T(4,128)(2,1)} %copy-done.8, bf16[8192,2048]{1,0:T(8,128)(2,1)S(1)} %shard_map.95.refs_0_), custom_call_target="tpu_custom_call", output_to_operand_aliasing={{}: (3, {})} | custom-call | bytes 5242880 | tf_op jit(solution)/shard_map/pallas_call | solution.py:76
  19.6 0.2 multiply_reduce_fusion
  20.0 1.6 %collective-permute-start.3 = (bf16[4,7296]{1,0:T(4,128)(2,1)S(1)}, bf16[4,7296]{1,0:T(4,128)(2,1)S(1)}, u32[]{:S(2)}, u32[]{:S(2)}) collective-permute-start(bf16[4,7296]{1,0:T(4,128)(2,1)S(1)} %maximum_maximum_fusion.after_ref), channel_id=1, source_target_pairs={{0,2},{1,3},{2,0},{3,1},{4,6},{5,7},{6,4},{7,5},{8,10},{9,11},{10,... | collective-permute-start | bytes 175112 | tf_op jit(solution)/shard_map/ppermute | solution.py:21
  21.6 2.2 %shard_map.97.refs_0_ = bf16[8192,2048]{1,0:T(8,128)(2,1)S(1)} custom-call(bf16[1,7168,2048]{2,1,0:T(8,128)(2,1)} %gate_hbm.13, bf16[1,7168,2048]{2,1,0:T(8,128)(2,1)} %up_hbm.15, bf16[4,7296]{1,0:T(4,128)(2,1)} %copy-done.9, bf16[8192,2048]{1,0:T(8,128)(2,1)S(1)} %shard_map.96.refs_0_), custom_call_target="tpu_custom_call", output_to_operand_aliasing={{}: (3, {})} | custom-call | bytes 4194304 | tf_op jit(solution)/shard_map/pallas_call | solution.py:76
  23.8 0.4 collective-permute-done.3
  24.3 0.8 %collective-permute-start.4 = (bf16[8,7296]{1,0:T(8,128)(2,1)S(1)}, bf16[8,7296]{1,0:T(8,128)(2,1)S(1)}, u32[]{:S(2)}, u32[]{:S(2)}) collective-permute-start(bf16[8,7296]{1,0:T(8,128)(2,1)S(1)} %pad_maximum_fusion.1.after_ref), channel_id=1, source_target_pairs={{0,1},{1,0},{2,3},{3,2},{4,5},{5,4},{6,7},{7,6},{8,9},{9,8},{10,11... | collective-permute-start | bytes 350216 | tf_op jit(solution)/shard_map/ppermute | solution.py:21
  25.1 3.1 %shard_map.98.refs_0_ = bf16[8192,2048]{1,0:T(8,128)(2,1)S(1)} custom-call(bf16[1,7168,2048]{2,1,0:T(8,128)(2,1)} %gate_hbm.13, bf16[1,7168,2048]{2,1,0:T(8,128)(2,1)} %up_hbm.15, bf16[8,7296]{1,0:T(8,128)(2,1)} %copy-done.7, bf16[8192,2048]{1,0:T(8,128)(2,1)S(1)} %shard_map.97.refs_0_), custom_call_target="tpu_custom_call", output_to_operand_aliasing={{}: (3, {})} | custom-call | bytes 7340032 | tf_op jit(solution)/shard_map/pallas_call | solution.py:76
  28.2 1.0 %collective-permute-done.4 = bf16[8,7296]{1,0:T(8,128)(2,1)S(1)} collective-permute-done((bf16[8,7296]{1,0:T(8,128)(2,1)S(1)}, bf16[8,7296]{1,0:T(8,128)(2,1)S(1)}, u32[]{:S(2)}, u32[]{:S(2)}) %collective-permute-start.4) | collective-permute-done | bytes 116768 | tf_op jit(solution)/shard_map/ppermute | solution.py:21
  29.2 0.1 pad_maximum_fusion.after_ref.own_ref
  29.4 0.6 copy-done.6
  30.0 1.9 %shard_map.99.held_ref = bf16[8192,2048]{1,0:T(8,128)(2,1)S(1)} custom-call(bf16[1,7168,2048]{2,1,0:T(8,128)(2,1)} %gate_hbm.13, bf16[1,7168,2048]{2,1,0:T(8,128)(2,1)} %up_hbm.15, bf16[16,7296]{1,0:T(8,128)(2,1)} %copy-done.6, bf16[8192,2048]{1,0:T(8,128)(2,1)S(1)} %shard_map.98.refs_0_), custom_call_target="tpu_custom_call", output_to_operand_aliasing={{}: (3, {})} | custom-call | bytes 3145728 | tf_op jit(solution)/shard_map/pallas_call | solution.py:76
  31.9 0.7 copy-done.10
  32.6 21.4 %shard_map.100 = (f32[16,7168]{1,0:T(8,128)}, bf16[16,7168]{1,0:T(8,128)(2,1)}) custom-call(bf16[16,7296]{1,0:T(8,128)(2,1)} %copy-done.6, bf16[16,7296]{1,0:T(8,128)(2,1)} %copy-done.10, bf16[8192,2048]{1,0:T(8,128)(2,1)S(1)} %shard_map.99.held_ref, bf16[1,7168,2048]{2,1,0:T(8,128)(2,1)} %up_hbm.15, bf16[1,2048,7168]{2,1,0:T(8,128)(2,1)} %down_hbm.1), custom_call_target="tpu_custom_call" | custom-call | flops 2818572288 | bytes 58720256 | tf_op jit(solution)/shard_map/pallas_call | solution.py:178
  54.1 1.7 %collective-permute-done.6 = bf16[16,7168]{1,0:T(8,128)(2,1)S(1)} collective-permute-done((bf16[16,7168]{1,0:T(8,128)(2,1)}, bf16[16,7168]{1,0:T(8,128)(2,1)S(1)}, u32[]{:S(2)}, u32[]{:S(2)}) %collective-permute-start.6) | collective-permute-done | bytes 229408 | tf_op jit(solution)/shard_map/ppermute | solution.py:21
  55.8 1.1 %convert_add_fusion = f32[16,7168]{1,0:T(8,128)S(1)} fusion(f32[16,7168]{1,0:T(8,128)} %get-tuple-element.41, bf16[16,7168]{1,0:T(8,128)(2,1)S(1)} %collective-permute-done.6), kind=kLoop, calls=%fused_computation | loop fusion | flops 229376 | bytes 1146880 | tf_op jit(solution)/shard_map/add | solution.py:243
  56.9 0.8 %collective-permute-start.7 = (bf16[8,7168]{1,0:T(8,128)(2,1)S(1)}, bf16[8,7168]{1,0:T(8,128)(2,1)S(1)}, u32[]{:S(2)}, u32[]{:S(2)}) collective-permute-start(bf16[8,7168]{1,0:T(8,128)(2,1)S(1)} %slice.93), channel_id=1, source_target_pairs={{0,1},{1,0},{2,3},{3,2},{4,5},{5,4},{6,7},{7,6},{8,9},{9,8},{10,11... | collective-permute-start | bytes 344072 | tf_op jit(solution)/shard_map/ppermute | solution.py:21
  57.7 4.4 %collective-permute-done.7 = bf16[8,7168]{1,0:T(8,128)(2,1)S(1)} collective-permute-done((bf16[8,7168]{1,0:T(8,128)(2,1)S(1)}, bf16[8,7168]{1,0:T(8,128)(2,1)S(1)}, u32[]{:S(2)}, u32[]{:S(2)}) %collective-permute-start.7) | collective-permute-done | bytes 114720 | tf_op jit(solution)/shard_map/ppermute | solution.py:21
  62.2 1.6 %collective-permute-start.8 = (bf16[4,7168]{1,0:T(4,128)(2,1)S(1)}, bf16[4,7168]{1,0:T(4,128)(2,1)S(1)}, u32[]{:S(2)}, u32[]{:S(2)}) collective-permute-start(bf16[4,7168]{1,0:T(4,128)(2,1)S(1)} %slice.94), channel_id=1, source_target_pairs={{0,2},{1,3},{2,0},{3,1},{4,6},{5,7},{6,4},{7,5},{8,10},{9,11},{10,... | collective-permute-start | bytes 172040 | tf_op jit(solution)/shard_map/ppermute | solution.py:21
  63.8 2.6 %collective-permute-done.8 = bf16[4,7168]{1,0:T(4,128)(2,1)S(1)} collective-permute-done((bf16[4,7168]{1,0:T(4,128)(2,1)S(1)}, bf16[4,7168]{1,0:T(4,128)(2,1)S(1)}, u32[]{:S(2)}, u32[]{:S(2)}) %collective-permute-start.8) | collective-permute-done | bytes 57376 | tf_op jit(solution)/shard_map/ppermute | solution.py:21
  66.5 2.7 %collective-permute-start.9 = (bf16[2,7168]{1,0:T(2,128)(2,1)S(1)}, bf16[2,7168]{1,0:T(2,128)(2,1)S(1)}, u32[]{:S(2)}, u32[]{:S(2)}) collective-permute-start(bf16[2,7168]{1,0:T(2,128)(2,1)S(1)} %slice.96), channel_id=1, source_target_pairs={{0,4},{1,5},{2,6},{3,7},{4,0},{5,1},{6,2},{7,3},{8,12},{9,13},{10,... | collective-permute-start | bytes 86024 | tf_op jit(solution)/shard_map/ppermute | solution.py:21
  69.3 2.1 %collective-permute-done.9 = bf16[2,7168]{1,0:T(2,128)(2,1)S(1)} collective-permute-done((bf16[2,7168]{1,0:T(2,128)(2,1)S(1)}, bf16[2,7168]{1,0:T(2,128)(2,1)S(1)}, u32[]{:S(2)}, u32[]{:S(2)}) %collective-permute-start.9) | collective-permute-done | bytes 28704 | tf_op jit(solution)/shard_map/ppermute | solution.py:21
  71.4 0.7 fusion.5
  (48 shorter events, 0.9 us)
Async XLA Ops:
  0.0 1.8 %copy-start.3 = (bf16[16,128]{1,0:T(8,128)(2,1)S(1)}, bf16[16,128]{1,0:T(8,128)(2,1)}, u32[]{:S(2)}) copy-start(bf16[16,128]{1,0:T(8,128)(2,1)} %attn_ref) | copy-start | bytes 12292
  0.0 2.1 %copy-start = (bf16[128,7168]{1,0:T(8,128)(2,1)S(1)}, bf16[128,7168]{1,0:T(8,128)(2,1)}, u32[]{:S(2)}) copy-start(bf16[128,7168]{1,0:T(8,128)(2,1)} %proj_ref.1) | copy-start | bytes 5505028
  2.6 3.1 %copy-start.1 = (bf16[8,7168]{1,0:T(8,128)(2,1)}, bf16[8,7168]{1,0:T(8,128)(2,1)S(1)}, u32[]{:S(2)}) copy-start(bf16[8,7168]{1,0:T(8,128)(2,1)S(1)} %get-tuple-element.26.after_ref) | copy-start | bytes 344068
  2.6 6.2 %copy-start.4 = (s32[2,8]{1,0:T(2,128)S(1)}, s32[2,8]{1,0:T(2,128)}, u32[]{:S(2)}) copy-start(s32[2,8]{1,0:T(2,128)} %routes_ref.1) | copy-start | bytes 196
  2.6 6.2 %copy-start.5 = (bf16[2,8]{1,0:T(2,128)(2,1)S(1)}, bf16[2,8]{1,0:T(2,128)(2,1)}, u32[]{:S(2)}) copy-start(bf16[2,8]{1,0:T(2,128)(2,1)} %route_w_ref.1) | copy-start | bytes 100
  2.6 7.2 %collective-permute-start = (bf16[8,7168]{1,0:T(8,128)(2,1)S(1)}, bf16[8,7168]{1,0:T(8,128)(2,1)S(1)}, u32[]{:S(2)}, u32[]{:S(2)}) collective-permute-start(bf16[8,7168]{1,0:T(8,128)(2,1)S(1)} %get-tuple-element.26.after_ref), channel_id=1, source_target_pairs={{0,1},{1,0},{2,3},{3,2},{4,5},{5,4},{6,7},{7,6},{8,9},{9,8},{10,11... | collective-permute-start | bytes 344072 | tf_op jit(solution)/shard_map/ppermute | solution.py:21
  8.8 0.9 %copy-start.2 = (bf16[8,7168]{1,0:T(8,128)(2,1)S(1)}, bf16[8,7168]{1,0:T(8,128)(2,1)}, u32[]{:S(2)}) copy-start(bf16[8,7168]{1,0:T(8,128)(2,1)} %copy-done.1) | copy-start | bytes 344068
  9.9 1.7 %copy-start.11 = (bf16[4,7168]{1,0:T(4,128)(2,1)}, bf16[4,7168]{1,0:T(4,128)(2,1)S(1)}, u32[]{:S(2)}) copy-start(bf16[4,7168]{1,0:T(4,128)(2,1)S(1)} %slice.95.after_ref) | copy-start | bytes 172036
  9.9 4.2 %collective-permute-start.1 = (bf16[4,7168]{1,0:T(4,128)(2,1)S(1)}, bf16[4,7168]{1,0:T(4,128)(2,1)S(1)}, u32[]{:S(2)}, u32[]{:S(2)}) collective-permute-start(bf16[4,7168]{1,0:T(4,128)(2,1)S(1)} %slice.95.after_ref), channel_id=1, source_target_pairs={{0,2},{1,3},{2,0},{3,1},{4,6},{5,7},{6,4},{7,5},{8,10},{9,11},{10,... | collective-permute-start | bytes 172040 | tf_op jit(solution)/shard_map/ppermute | solution.py:21
  11.5 2.6 %copy-start.13 = (bf16[2,7168]{1,0:T(2,128)(2,1)S(1)}, bf16[2,7168]{1,0:T(2,128)(2,1)}, u32[]{:S(2)}) copy-start(bf16[2,7168]{1,0:T(2,128)(2,1)} %param.11) | copy-start | bytes 86020
  14.3 2.7 %copy-start.8 = (bf16[4,7296]{1,0:T(4,128)(2,1)}, bf16[4,7296]{1,0:T(4,128)(2,1)S(1)}, u32[]{:S(2)}) copy-start(bf16[4,7296]{1,0:T(4,128)(2,1)S(1)} %fusion.3.after_ref) | copy-start | bytes 175108
  14.3 5.5 %copy-start.12 = (f32[7168]{0:T(1024)S(1)}, f32[7168]{0:T(1024)}, u32[]{:S(2)}) copy-start(f32[7168]{0:T(1024)} %param.12) | copy-start | bytes 86020
  14.3 5.2 %collective-permute-start.2 = (bf16[4,7296]{1,0:T(4,128)(2,1)S(1)}, bf16[4,7296]{1,0:T(4,128)(2,1)S(1)}, u32[]{:S(2)}, u32[]{:S(2)}) collective-permute-start(bf16[4,7296]{1,0:T(4,128)(2,1)S(1)} %fusion.3.after_ref), channel_id=1, source_target_pairs={{0,4},{1,5},{2,6},{3,7},{4,0},{5,1},{6,2},{7,3},{8,12},{9,13},{10,... | collective-permute-start | bytes 175112 | tf_op jit(solution)/shard_map/ppermute | solution.py:21
  20.0 1.7 %copy-start.9 = (bf16[4,7296]{1,0:T(4,128)(2,1)}, bf16[4,7296]{1,0:T(4,128)(2,1)S(1)}, u32[]{:S(2)}) copy-start(bf16[4,7296]{1,0:T(4,128)(2,1)S(1)} %maximum_maximum_fusion.after_ref) | copy-start | bytes 175108
  20.0 4.3 %collective-permute-start.3 = (bf16[4,7296]{1,0:T(4,128)(2,1)S(1)}, bf16[4,7296]{1,0:T(4,128)(2,1)S(1)}, u32[]{:S(2)}, u32[]{:S(2)}) collective-permute-start(bf16[4,7296]{1,0:T(4,128)(2,1)S(1)} %maximum_maximum_fusion.after_ref), channel_id=1, source_target_pairs={{0,2},{1,3},{2,0},{3,1},{4,6},{5,7},{6,4},{7,5},{8,10},{9,11},{10,... | collective-permute-start | bytes 175112 | tf_op jit(solution)/shard_map/ppermute | solution.py:21
  24.3 0.8 %copy-start.7 = (bf16[8,7296]{1,0:T(8,128)(2,1)}, bf16[8,7296]{1,0:T(8,128)(2,1)S(1)}, u32[]{:S(2)}) copy-start(bf16[8,7296]{1,0:T(8,128)(2,1)S(1)} %pad_maximum_fusion.1.after_ref) | copy-start | bytes 350212
  24.3 4.9 %collective-permute-start.4 = (bf16[8,7296]{1,0:T(8,128)(2,1)S(1)}, bf16[8,7296]{1,0:T(8,128)(2,1)S(1)}, u32[]{:S(2)}, u32[]{:S(2)}) collective-permute-start(bf16[8,7296]{1,0:T(8,128)(2,1)S(1)} %pad_maximum_fusion.1.after_ref), channel_id=1, source_target_pairs={{0,1},{1,0},{2,3},{3,2},{4,5},{5,4},{6,7},{7,6},{8,9},{9,8},{10,11... | collective-permute-start | bytes 350216 | tf_op jit(solution)/shard_map/ppermute | solution.py:21
  29.3 0.7 copy-start.6
  29.3 2.6 %collective-permute-start.5 = (bf16[16,7296]{1,0:T(8,128)(2,1)S(1)}, bf16[16,7296]{1,0:T(8,128)(2,1)S(1)}, u32[]{:S(2)}, u32[]{:S(2)}) collective-permute-start(bf16[16,7296]{1,0:T(8,128)(2,1)S(1)} %pad_maximum_fusion.after_ref.own_ref), channel_id=1, source_target_pairs={{0,8},{8,0},{1,9},{9,1},{2,10},{10,2},{3,11},{11,3},{4,12},{12,4},... | collective-permute-start | bytes 700424 | tf_op jit(solution)/shard_map/ppermute | solution.py:21
  31.9 0.7 copy-start.10
  54.0 1.8 %collective-permute-start.6 = (bf16[16,7168]{1,0:T(8,128)(2,1)}, bf16[16,7168]{1,0:T(8,128)(2,1)S(1)}, u32[]{:S(2)}, u32[]{:S(2)}) collective-permute-start(bf16[16,7168]{1,0:T(8,128)(2,1)} %get-tuple-element.42), channel_id=1, source_target_pairs={{0,8},{8,0},{1,9},{9,1},{2,10},{10,2},{3,11},{11,3},{4,12},{12,4},... | collective-permute-start | bytes 688136 | tf_op jit(solution)/shard_map/ppermute | solution.py:21
  56.9 5.3 %collective-permute-start.7 = (bf16[8,7168]{1,0:T(8,128)(2,1)S(1)}, bf16[8,7168]{1,0:T(8,128)(2,1)S(1)}, u32[]{:S(2)}, u32[]{:S(2)}) collective-permute-start(bf16[8,7168]{1,0:T(8,128)(2,1)S(1)} %slice.93), channel_id=1, source_target_pairs={{0,1},{1,0},{2,3},{3,2},{4,5},{5,4},{6,7},{7,6},{8,9},{9,8},{10,11... | collective-permute-start | bytes 344072 | tf_op jit(solution)/shard_map/ppermute | solution.py:21
  62.2 4.2 %collective-permute-start.8 = (bf16[4,7168]{1,0:T(4,128)(2,1)S(1)}, bf16[4,7168]{1,0:T(4,128)(2,1)S(1)}, u32[]{:S(2)}, u32[]{:S(2)}) collective-permute-start(bf16[4,7168]{1,0:T(4,128)(2,1)S(1)} %slice.94), channel_id=1, source_target_pairs={{0,2},{1,3},{2,0},{3,1},{4,6},{5,7},{6,4},{7,5},{8,10},{9,11},{10,... | collective-permute-start | bytes 172040 | tf_op jit(solution)/shard_map/ppermute | solution.py:21
  66.5 4.8 %collective-permute-start.9 = (bf16[2,7168]{1,0:T(2,128)(2,1)S(1)}, bf16[2,7168]{1,0:T(2,128)(2,1)S(1)}, u32[]{:S(2)}, u32[]{:S(2)}) collective-permute-start(bf16[2,7168]{1,0:T(2,128)(2,1)S(1)} %slice.96), channel_id=1, source_target_pairs={{0,4},{1,5},{2,6},{3,7},{4,0},{5,1},{6,2},{7,3},{8,12},{9,13},{10,... | collective-permute-start | bytes 86024 | tf_op jit(solution)/shard_map/ppermute | solution.py:21

commit v3 on v2

--- a/solution.py
+++ b/solution.py
@@ -25,7 +25,8 @@
     return pltpu.with_memory_space_constraint(x, pltpu.VMEM)
 
 
-def project_kernel(n_local, tok_rows, attn_ref, proj_ref, keep_ref, send_ref):
+def project_kernel(n_local, attn_ref, proj_ref, routes_ref, route_w_ref, keep_ref, send_ref, picks_ref):
+    tok_rows, top = routes_ref.shape
     count = n_local * tok_rows
     here = lax.axis_index("local")
     place = lax.broadcasted_iota(jnp.int32, (count, count), 0)
@@ -40,18 +41,28 @@
     partial = jnp.dot(ordered, proj_ref[...], preferred_element_type=F32)
     keep_ref[...] = partial[:half]
     send_ref[...] = partial[half:].astype(BF16)
-
-
-def project(attn_out, o_proj, tok_rows):
+    lane = lax.broadcasted_iota(jnp.int32, (tok_rows, LANES), 1)
+    total = jnp.zeros((tok_rows, LANES), F32)
+    weights = route_w_ref[...].astype(F32)
+    for k in range(top):
+        total = total + jnp.where(routes_ref[:, k : k + 1] == lane, weights[:, k : k + 1], 0.0)
+    picks_ref[...] = total
+
+
+def project(attn_out, o_proj, routes, route_w):
     depth = o_proj.shape[1]
     half = attn_out.shape[0] // 2
     return pl.pallas_call(
-        functools.partial(project_kernel, lax.axis_size("local"), tok_rows),
-        out_shape=(pltpu.VMEM((half, depth), F32), pltpu.VMEM((half, depth), BF16)),
-        in_specs=[VMEM, VMEM],
-        out_specs=(VMEM, VMEM),
+        functools.partial(project_kernel, lax.axis_size("local")),
+        out_shape=(
+            pltpu.VMEM((half, depth), F32),
+            pltpu.VMEM((half, depth), BF16),
+            pltpu.VMEM((routes.shape[0], LANES), F32),
+        ),
+        in_specs=[VMEM] * 4,
+        out_specs=(VMEM, VMEM, VMEM),
         compiler_params=pltpu.CompilerParams(vmem_limit_bytes=VMEM_OWN),
-    )(attn_out, o_proj)
+    )(attn_out, o_proj, routes, route_w)
 
 
 def fetch_kernel(depth, first, last, gate_hbm, up_hbm, after_ref, *refs):
@@ -83,26 +94,6 @@
         compiler_params=pltpu.CompilerParams(vmem_limit_bytes=VMEM_OWN),
         cost_estimate=pl.CostEstimate(flops=0, bytes_accessed=2 * (last - first) * width, transcendentals=0),
     )(w_gate, w_up, after, *kept)
-
-
-def picks_kernel(routes_ref, route_w_ref, after_ref, picks_ref):
-    tok_rows, top = routes_ref.shape
-    lane = lax.broadcasted_iota(jnp.int32, (tok_rows, LANES), 1)
-    total = jnp.zeros((tok_rows, LANES), F32)
-    weights = route_w_ref[...].astype(F32)
-    for k in range(top):
-        total = total + jnp.where(routes_ref[:, k : k + 1] == lane, weights[:, k : k + 1], 0.0)
-    picks_ref[...] = total
-
-
-def picks_of(routes, route_w, after):
-    return pl.pallas_call(
-        picks_kernel,
-        out_shape=pltpu.VMEM((routes.shape[0], LANES), F32),
-        in_specs=[VMEM, VMEM, ANYWHERE],
-        out_specs=VMEM,
-        compiler_params=pltpu.CompilerParams(vmem_limit_bytes=VMEM_OWN),
-    )(routes, route_w, after)
 
 
 def expert_kernel(
@@ -164,7 +155,7 @@
                 gate_val = acc_g[...]
                 act_ref[...] = (gate_val / (1.0 + jnp.exp(-gate_val)) * acc_u[...]).astype(BF16)
             piece = jnp.dot(act_ref[...], ring[slot], preferred_element_type=F32) * coeff
-            keep_ref[:, pl.ds(at, chunk)] = piece[:half]
+            keep_ref[:, pl.ds(at, chunk)] = piece[:half].astype(BF16)
             send_ref[:, pl.ds(at, chunk)] = piece[half:].astype(BF16)
         if step + slots < len(steps):
             start(step + slots)
@@ -177,7 +168,7 @@
     slots = SLOTS
     return pl.pallas_call(
         functools.partial(expert_kernel, lax.axis_size("local"), chunk),
-        out_shape=(jax.ShapeDtypeStruct((half, depth), F32), jax.ShapeDtypeStruct((half, depth), BF16)),
+        out_shape=(jax.ShapeDtypeStruct((half, depth), BF16), jax.ShapeDtypeStruct((half, depth), BF16)),
         in_specs=[VMEM, VMEM, VMEM, ANYWHERE, ANYWHERE],
         out_specs=(VMEM, VMEM),
         scratch_shapes=[
@@ -210,16 +201,16 @@
     held, step = fetch(w_gate, w_up, None, total, 0, cuts[1], attn_out), 1
     attn_out, held = lax.optimization_barrier((attn_out, held))
 
-    def send(x, axis, bit, more=()):
+    def send(x, axis, bit):
         nonlocal held, step
         got = swap(x, axis, bit)
         held = fetch(w_gate, w_up, held, total, cuts[step], cuts[step + 1], x)
-        got, held, *more = lax.optimization_barrier((got, held, *more))
+        got, held = lax.optimization_barrier((got, held))
         step += 1
-        return (got, *more) if more else got
-
-    keep, away = project(attn_out, o_proj, tok_rows)
-    got, picks = send(away, "local", bits[0], (picks_of(routes, route_w, away),))
+        return got
+
+    keep, away, picks = project(attn_out, o_proj, routes, route_w)
+    got = send(away, "local", bits[0])
     partial = keep + got.astype(F32)
     for bit in bits[1:-1]:
         half = partial.shape[0] // 2
@@ -240,7 +231,7 @@
     other = send(tokens, "node", 1)
 
     keep, away = expert(tokens, other, held, w_up, w_down, chunk)
-    keep = keep + swap(away, "node", 1).astype(F32)
+    keep = keep.astype(F32) + swap(away, "node", 1).astype(F32)
     for bit in bits:
         half = keep.shape[0] // 2
         keep = keep[:half] + swap(keep[half:].astype(BF16), "local", bit).astype(F32)

time: 72.4 us -> 71.3 us (0.985)
  starting transfers between devices: 15.1 us -> 17.1 us
  waiting for transfers between devices: 12.6 us -> 10.9 us
  local copies, waits for them, and re-layouts: 2.75 us -> 1.86 us
    ppermute x10, starting transfers between devices: 15.1 us -> 17.1 us  [swap(): lax.ppermute(x, axis, [(i, i ^ bit) for i in range(lax.axis_size(axis))])]
    ppermute x10, waiting for transfers between devices: 12.6 us -> 10.9 us  [swap(): lax.ppermute(x, axis, [(i, i ^ bit) for i in range(lax.axis_size(axis))])]
    unnamed x28 -> x26, local copies, waits for them, and re-layouts: 2.6 us -> 1.72 us
where the time goes in v3:
time: 71.3 us; the launch traced here: 71 us
  Pallas kernels  38.5 us (54%)
  starting transfers between devices  17.1 us (24%)
  waiting for transfers between devices  10.9 us (15%)
  other arithmetic  2.43 us (3%)
  local copies, waits for them, and re-layouts  1.86 us (3%)
    pallas_call x1, Pallas kernels, expert(): pl.pallas_call(functools.partial(expert_kernel, lax.axis_size('local'), c...  21.3 us
    ppermute x10, starting transfers between devices, swap(): lax.ppermute(x, axis, [(i, i ^ bit) for i in range(lax.axis_size(axis))])  17.1 us
    pallas_call x7, Pallas kernels, fetch(): pl.pallas_call(functools.partial(fetch_kernel, depth, first, last), out_s...  16.7 us
    ppermute x10, waiting for transfers between devices, swap(): lax.ppermute(x, axis, [(i, i ^ bit) for i in range(lax.axis_size(axis))])  10.9 us
    unnamed x26, local copies, waits for them, and re-layouts  1.72 us
  transfers between devices with their start and end apart: 10, of which 7 were waited for; matrix products, arithmetic and copies ran while one was open for 0% of the time, Pallas kernels for 21%

profile of v3, /device:TPU:0, one launch (start us, length us, event | category | flops | bytes accessed | tf_op | source)
XLA Modules:
  0.0 71.0 jit_solution(15500186581611080059)
XLA Ops:
  0.0 1.7 %shard_map.91.refs_0_ = bf16[8192,2048]{1,0:T(8,128)(2,1)S(1)} custom-call(bf16[1,7168,2048]{2,1,0:T(8,128)(2,1)} %gate_hbm.13, bf16[1,7168,2048]{2,1,0:T(8,128)(2,1)} %up_hbm.15, bf16[16,128]{1,0:T(8,128)(2,1)} %attn_ref), custom_call_target="tpu_custom_call" | custom-call | bytes 2097152 | tf_op jit(solution)/shard_map/pallas_call | solution.py:87
  1.8 0.4 copy-done
  2.2 0.5 shard_map.92
  2.6 3.0 %collective-permute-start = (bf16[8,7168]{1,0:T(8,128)(2,1)S(1)}, bf16[8,7168]{1,0:T(8,128)(2,1)S(1)}, u32[]{:S(2)}, u32[]{:S(2)}) collective-permute-start(bf16[8,7168]{1,0:T(8,128)(2,1)S(1)} %get-tuple-element.26.after_ref), channel_id=1, source_target_pairs={{0,1},{1,0},{2,3},{3,2},{4,5},{5,4},{6,7},{7,6},{8,9},{9,8},{10,11... | collective-permute-start | bytes 344072 | tf_op jit(solution)/shard_map/ppermute | solution.py:21
  5.7 3.1 %shard_map.93.refs_0_ = bf16[8192,2048]{1,0:T(8,128)(2,1)S(1)} custom-call(bf16[1,7168,2048]{2,1,0:T(8,128)(2,1)} %gate_hbm.13, bf16[1,7168,2048]{2,1,0:T(8,128)(2,1)} %up_hbm.15, bf16[8,7168]{1,0:T(8,128)(2,1)} %copy-done.1, bf16[8192,2048]{1,0:T(8,128)(2,1)S(1)} %shard_map.91.refs_0_), custom_call_target="tpu_custom_call", output_to_operand_aliasing={{}: (3, {})} | custom-call | bytes 7340032 | tf_op jit(solution)/shard_map/pallas_call | solution.py:87
  8.9 1.9 %collective-permute-start.1 = (bf16[4,7168]{1,0:T(4,128)(2,1)S(1)}, bf16[4,7168]{1,0:T(4,128)(2,1)S(1)}, u32[]{:S(2)}, u32[]{:S(2)}) collective-permute-start(bf16[4,7168]{1,0:T(4,128)(2,1)S(1)} %slice.95.after_ref), channel_id=1, source_target_pairs={{0,2},{1,3},{2,0},{3,1},{4,6},{5,7},{6,4},{7,5},{8,10},{9,11},{10,... | collective-permute-start | bytes 172040 | tf_op jit(solution)/shard_map/ppermute | solution.py:21
  10.8 2.2 %shard_map.94.refs_0_ = bf16[8192,2048]{1,0:T(8,128)(2,1)S(1)} custom-call(bf16[1,7168,2048]{2,1,0:T(8,128)(2,1)} %gate_hbm.13, bf16[1,7168,2048]{2,1,0:T(8,128)(2,1)} %up_hbm.15, bf16[4,7168]{1,0:T(4,128)(2,1)} %copy-done.10, bf16[8192,2048]{1,0:T(8,128)(2,1)S(1)} %shard_map.93.refs_0_), custom_call_target="tpu_custom_call", output_to_operand_aliasing={{}: (3, {})} | custom-call | bytes 4194304 | tf_op jit(solution)/shard_map/pallas_call | solution.py:87
  13.0 0.2 collective-permute-done.1
  13.3 2.9 %collective-permute-start.2 = (bf16[4,7296]{1,0:T(4,128)(2,1)S(1)}, bf16[4,7296]{1,0:T(4,128)(2,1)S(1)}, u32[]{:S(2)}, u32[]{:S(2)}) collective-permute-start(bf16[4,7296]{1,0:T(4,128)(2,1)S(1)} %fusion.3.after_ref), channel_id=1, source_target_pairs={{0,4},{1,5},{2,6},{3,7},{4,0},{5,1},{6,2},{7,3},{8,12},{9,13},{10,... | collective-permute-start | bytes 175112 | tf_op jit(solution)/shard_map/ppermute | solution.py:21
  16.2 2.5 %shard_map.95.refs_0_ = bf16[8192,2048]{1,0:T(8,128)(2,1)S(1)} custom-call(bf16[1,7168,2048]{2,1,0:T(8,128)(2,1)} %gate_hbm.13, bf16[1,7168,2048]{2,1,0:T(8,128)(2,1)} %up_hbm.15, bf16[4,7296]{1,0:T(4,128)(2,1)} %copy-done.7, bf16[8192,2048]{1,0:T(8,128)(2,1)S(1)} %shard_map.94.refs_0_), custom_call_target="tpu_custom_call", output_to_operand_aliasing={{}: (3, {})} | custom-call | bytes 5242880 | tf_op jit(solution)/shard_map/pallas_call | solution.py:87
  18.8 0.2 multiply_reduce_fusion
  19.0 0.1 multiply_convert_fusion
  19.2 1.6 %collective-permute-start.3 = (bf16[4,7296]{1,0:T(4,128)(2,1)S(1)}, bf16[4,7296]{1,0:T(4,128)(2,1)S(1)}, u32[]{:S(2)}, u32[]{:S(2)}) collective-permute-start(bf16[4,7296]{1,0:T(4,128)(2,1)S(1)} %maximum_maximum_fusion.after_ref), channel_id=1, source_target_pairs={{0,2},{1,3},{2,0},{3,1},{4,6},{5,7},{6,4},{7,5},{8,10},{9,11},{10,... | collective-permute-start | bytes 175112 | tf_op jit(solution)/shard_map/ppermute | solution.py:21
  20.8 2.2 %shard_map.96.refs_0_ = bf16[8192,2048]{1,0:T(8,128)(2,1)S(1)} custom-call(bf16[1,7168,2048]{2,1,0:T(8,128)(2,1)} %gate_hbm.13, bf16[1,7168,2048]{2,1,0:T(8,128)(2,1)} %up_hbm.15, bf16[4,7296]{1,0:T(4,128)(2,1)} %copy-done.8, bf16[8192,2048]{1,0:T(8,128)(2,1)S(1)} %shard_map.95.refs_0_), custom_call_target="tpu_custom_call", output_to_operand_aliasing={{}: (3, {})} | custom-call | bytes 4194304 | tf_op jit(solution)/shard_map/pallas_call | solution.py:87
  23.1 0.4 collective-permute-done.3
  23.5 1.6 %collective-permute-start.4 = (bf16[8,7296]{1,0:T(8,128)(2,1)S(1)}, bf16[8,7296]{1,0:T(8,128)(2,1)S(1)}, u32[]{:S(2)}, u32[]{:S(2)}) collective-permute-start(bf16[8,7296]{1,0:T(8,128)(2,1)S(1)} %pad_maximum_fusion.1.after_ref), channel_id=1, source_target_pairs={{0,1},{1,0},{2,3},{3,2},{4,5},{5,4},{6,7},{7,6},{8,9},{9,8},{10,11... | collective-permute-start | bytes 350216 | tf_op jit(solution)/shard_map/ppermute | solution.py:21
  25.1 3.1 %shard_map.97.refs_0_ = bf16[8192,2048]{1,0:T(8,128)(2,1)S(1)} custom-call(bf16[1,7168,2048]{2,1,0:T(8,128)(2,1)} %gate_hbm.13, bf16[1,7168,2048]{2,1,0:T(8,128)(2,1)} %up_hbm.15, bf16[8,7296]{1,0:T(8,128)(2,1)} %copy-done.6, bf16[8192,2048]{1,0:T(8,128)(2,1)S(1)} %shard_map.96.refs_0_), custom_call_target="tpu_custom_call", output_to_operand_aliasing={{}: (3, {})} | custom-call | bytes 7340032 | tf_op jit(solution)/shard_map/pallas_call | solution.py:87
  28.2 0.2 collective-permute-done.4
  28.4 0.1 pad_maximum_fusion.after_ref.own_ref
  28.6 0.6 copy-done.5
  29.2 1.9 %shard_map.98.held_ref = bf16[8192,2048]{1,0:T(8,128)(2,1)S(1)} custom-call(bf16[1,7168,2048]{2,1,0:T(8,128)(2,1)} %gate_hbm.13, bf16[1,7168,2048]{2,1,0:T(8,128)(2,1)} %up_hbm.15, bf16[16,7296]{1,0:T(8,128)(2,1)} %copy-done.5, bf16[8192,2048]{1,0:T(8,128)(2,1)S(1)} %shard_map.97.refs_0_), custom_call_target="tpu_custom_call", output_to_operand_aliasing={{}: (3, {})} | custom-call | bytes 3145728 | tf_op jit(solution)/shard_map/pallas_call | solution.py:87
  31.1 0.7 copy-done.9
  31.8 21.3 %shard_map.99 = (bf16[16,7168]{1,0:T(8,128)(2,1)}, bf16[16,7168]{1,0:T(8,128)(2,1)}) custom-call(bf16[16,7296]{1,0:T(8,128)(2,1)} %copy-done.5, bf16[16,7296]{1,0:T(8,128)(2,1)} %copy-done.9, bf16[8192,2048]{1,0:T(8,128)(2,1)S(1)} %shard_map.98.held_ref, bf16[1,7168,2048]{2,1,0:T(8,128)(2,1)} %up_hbm.15, bf16[1,2048,7168]{2,1,0:T(8,128)(2,1)} %down_hbm.1), custom_call_target="tpu_custom_call" | custom-call | flops 2818572288 | bytes 58720256 | tf_op jit(solution)/shard_map/pallas_call | solution.py:169
  53.2 1.7 %collective-permute-done.6 = bf16[16,7168]{1,0:T(8,128)(2,1)S(1)} collective-permute-done((bf16[16,7168]{1,0:T(8,128)(2,1)}, bf16[16,7168]{1,0:T(8,128)(2,1)S(1)}, u32[]{:S(2)}, u32[]{:S(2)}) %collective-permute-start.6) | collective-permute-done | bytes 229408 | tf_op jit(solution)/shard_map/ppermute | solution.py:21
  54.9 1.0 %convert_add_fusion = f32[16,7168]{1,0:T(8,128)S(1)} fusion(bf16[16,7168]{1,0:T(8,128)(2,1)S(1)} %collective-permute-done.6, bf16[16,7168]{1,0:T(8,128)(2,1)} %get-tuple-element.41), kind=kLoop, calls=%fused_computation | loop fusion | flops 344064 | bytes 917504 | tf_op jit(solution)/shard_map/add | solution.py:234
  55.9 1.6 %collective-permute-start.7 = (bf16[8,7168]{1,0:T(8,128)(2,1)S(1)}, bf16[8,7168]{1,0:T(8,128)(2,1)S(1)}, u32[]{:S(2)}, u32[]{:S(2)}) collective-permute-start(bf16[8,7168]{1,0:T(8,128)(2,1)S(1)} %slice.93), channel_id=1, source_target_pairs={{0,1},{1,0},{2,3},{3,2},{4,5},{5,4},{6,7},{7,6},{8,9},{9,8},{10,11... | collective-permute-start | bytes 344072 | tf_op jit(solution)/shard_map/ppermute | solution.py:21
  57.5 3.7 %collective-permute-done.7 = bf16[8,7168]{1,0:T(8,128)(2,1)S(1)} collective-permute-done((bf16[8,7168]{1,0:T(8,128)(2,1)S(1)}, bf16[8,7168]{1,0:T(8,128)(2,1)S(1)}, u32[]{:S(2)}, u32[]{:S(2)}) %collective-permute-start.7) | collective-permute-done | bytes 114720 | tf_op jit(solution)/shard_map/ppermute | solution.py:21
  61.2 1.6 %collective-permute-start.8 = (bf16[4,7168]{1,0:T(4,128)(2,1)S(1)}, bf16[4,7168]{1,0:T(4,128)(2,1)S(1)}, u32[]{:S(2)}, u32[]{:S(2)}) collective-permute-start(bf16[4,7168]{1,0:T(4,128)(2,1)S(1)} %slice.94), channel_id=1, source_target_pairs={{0,2},{1,3},{2,0},{3,1},{4,6},{5,7},{6,4},{7,5},{8,10},{9,11},{10,... | collective-permute-start | bytes 172040 | tf_op jit(solution)/shard_map/ppermute | solution.py:21
  62.9 2.6 %collective-permute-done.8 = bf16[4,7168]{1,0:T(4,128)(2,1)S(1)} collective-permute-done((bf16[4,7168]{1,0:T(4,128)(2,1)S(1)}, bf16[4,7168]{1,0:T(4,128)(2,1)S(1)}, u32[]{:S(2)}, u32[]{:S(2)}) %collective-permute-start.8) | collective-permute-done | bytes 57376 | tf_op jit(solution)/shard_map/ppermute | solution.py:21
  65.5 2.7 %collective-permute-start.9 = (bf16[2,7168]{1,0:T(2,128)(2,1)S(1)}, bf16[2,7168]{1,0:T(2,128)(2,1)S(1)}, u32[]{:S(2)}, u32[]{:S(2)}) collective-permute-start(bf16[2,7168]{1,0:T(2,128)(2,1)S(1)} %slice.96), channel_id=1, source_target_pairs={{0,4},{1,5},{2,6},{3,7},{4,0},{5,1},{6,2},{7,3},{8,12},{9,13},{10,... | collective-permute-start | bytes 86024 | tf_op jit(solution)/shard_map/ppermute | solution.py:21
  68.3 2.1 %collective-permute-done.9 = bf16[2,7168]{1,0:T(2,128)(2,1)S(1)} collective-permute-done((bf16[2,7168]{1,0:T(2,128)(2,1)S(1)}, bf16[2,7168]{1,0:T(2,128)(2,1)S(1)}, u32[]{:S(2)}, u32[]{:S(2)}) %collective-permute-start.9) | collective-permute-done | bytes 28704 | tf_op jit(solution)/shard_map/ppermute | solution.py:21
  70.4 0.7 fusion.5
  (45 shorter events, 0.7 us)
Async XLA Ops:
  0.0 1.8 %copy-start.2 = (bf16[16,128]{1,0:T(8,128)(2,1)S(1)}, bf16[16,128]{1,0:T(8,128)(2,1)}, u32[]{:S(2)}) copy-start(bf16[16,128]{1,0:T(8,128)(2,1)} %attn_ref) | copy-start | bytes 12292
  0.0 1.8 %copy-start.4 = (bf16[2,8]{1,0:T(2,128)(2,1)S(1)}, bf16[2,8]{1,0:T(2,128)(2,1)}, u32[]{:S(2)}) copy-start(bf16[2,8]{1,0:T(2,128)(2,1)} %route_w_ref.1) | copy-start | bytes 100
  0.0 1.8 %copy-start.3 = (s32[2,8]{1,0:T(2,128)S(1)}, s32[2,8]{1,0:T(2,128)}, u32[]{:S(2)}) copy-start(s32[2,8]{1,0:T(2,128)} %routes_ref.1) | copy-start | bytes 196
  0.0 2.2 %copy-start = (bf16[128,7168]{1,0:T(8,128)(2,1)S(1)}, bf16[128,7168]{1,0:T(8,128)(2,1)}, u32[]{:S(2)}) copy-start(bf16[128,7168]{1,0:T(8,128)(2,1)} %proj_ref.1) | copy-start | bytes 5505028
  2.6 3.0 %copy-start.1 = (bf16[8,7168]{1,0:T(8,128)(2,1)}, bf16[8,7168]{1,0:T(8,128)(2,1)S(1)}, u32[]{:S(2)}) copy-start(bf16[8,7168]{1,0:T(8,128)(2,1)S(1)} %get-tuple-element.26.after_ref) | copy-start | bytes 344068
  2.6 6.2 %collective-permute-start = (bf16[8,7168]{1,0:T(8,128)(2,1)S(1)}, bf16[8,7168]{1,0:T(8,128)(2,1)S(1)}, u32[]{:S(2)}, u32[]{:S(2)}) collective-permute-start(bf16[8,7168]{1,0:T(8,128)(2,1)S(1)} %get-tuple-element.26.after_ref), channel_id=1, source_target_pairs={{0,1},{1,0},{2,3},{3,2},{4,5},{5,4},{6,7},{7,6},{8,9},{9,8},{10,11... | collective-permute-start | bytes 344072 | tf_op jit(solution)/shard_map/ppermute | solution.py:21
  8.9 1.9 %copy-start.10 = (bf16[4,7168]{1,0:T(4,128)(2,1)}, bf16[4,7168]{1,0:T(4,128)(2,1)S(1)}, u32[]{:S(2)}) copy-start(bf16[4,7168]{1,0:T(4,128)(2,1)S(1)} %slice.95.after_ref) | copy-start | bytes 172036
  8.9 4.2 %collective-permute-start.1 = (bf16[4,7168]{1,0:T(4,128)(2,1)S(1)}, bf16[4,7168]{1,0:T(4,128)(2,1)S(1)}, u32[]{:S(2)}, u32[]{:S(2)}) collective-permute-start(bf16[4,7168]{1,0:T(4,128)(2,1)S(1)} %slice.95.after_ref), channel_id=1, source_target_pairs={{0,2},{1,3},{2,0},{3,1},{4,6},{5,7},{6,4},{7,5},{8,10},{9,11},{10,... | collective-permute-start | bytes 172040 | tf_op jit(solution)/shard_map/ppermute | solution.py:21
  10.7 2.4 %copy-start.12 = (bf16[2,7168]{1,0:T(2,128)(2,1)S(1)}, bf16[2,7168]{1,0:T(2,128)(2,1)}, u32[]{:S(2)}) copy-start(bf16[2,7168]{1,0:T(2,128)(2,1)} %param.11) | copy-start | bytes 86020
  13.3 2.9 %copy-start.7 = (bf16[4,7296]{1,0:T(4,128)(2,1)}, bf16[4,7296]{1,0:T(4,128)(2,1)S(1)}, u32[]{:S(2)}) copy-start(bf16[4,7296]{1,0:T(4,128)(2,1)S(1)} %fusion.3.after_ref) | copy-start | bytes 175108
  13.3 5.7 %copy-start.11 = (f32[7168]{0:T(1024)S(1)}, f32[7168]{0:T(1024)}, u32[]{:S(2)}) copy-start(f32[7168]{0:T(1024)} %param.12) | copy-start | bytes 86020
  13.3 5.4 %collective-permute-start.2 = (bf16[4,7296]{1,0:T(4,128)(2,1)S(1)}, bf16[4,7296]{1,0:T(4,128)(2,1)S(1)}, u32[]{:S(2)}, u32[]{:S(2)}) collective-permute-start(bf16[4,7296]{1,0:T(4,128)(2,1)S(1)} %fusion.3.after_ref), channel_id=1, source_target_pairs={{0,4},{1,5},{2,6},{3,7},{4,0},{5,1},{6,2},{7,3},{8,12},{9,13},{10,... | collective-permute-start | bytes 175112 | tf_op jit(solution)/shard_map/ppermute | solution.py:21
  19.2 1.7 %copy-start.8 = (bf16[4,7296]{1,0:T(4,128)(2,1)}, bf16[4,7296]{1,0:T(4,128)(2,1)S(1)}, u32[]{:S(2)}) copy-start(bf16[4,7296]{1,0:T(4,128)(2,1)S(1)} %maximum_maximum_fusion.after_ref) | copy-start | bytes 175108
  19.2 4.3 %collective-permute-start.3 = (bf16[4,7296]{1,0:T(4,128)(2,1)S(1)}, bf16[4,7296]{1,0:T(4,128)(2,1)S(1)}, u32[]{:S(2)}, u32[]{:S(2)}) collective-permute-start(bf16[4,7296]{1,0:T(4,128)(2,1)S(1)} %maximum_maximum_fusion.after_ref), channel_id=1, source_target_pairs={{0,2},{1,3},{2,0},{3,1},{4,6},{5,7},{6,4},{7,5},{8,10},{9,11},{10,... | collective-permute-start | bytes 175112 | tf_op jit(solution)/shard_map/ppermute | solution.py:21
  23.5 1.6 %copy-start.6 = (bf16[8,7296]{1,0:T(8,128)(2,1)}, bf16[8,7296]{1,0:T(8,128)(2,1)S(1)}, u32[]{:S(2)}) copy-start(bf16[8,7296]{1,0:T(8,128)(2,1)S(1)} %pad_maximum_fusion.1.after_ref) | copy-start | bytes 350212
  23.5 4.9 %collective-permute-start.4 = (bf16[8,7296]{1,0:T(8,128)(2,1)S(1)}, bf16[8,7296]{1,0:T(8,128)(2,1)S(1)}, u32[]{:S(2)}, u32[]{:S(2)}) collective-permute-start(bf16[8,7296]{1,0:T(8,128)(2,1)S(1)} %pad_maximum_fusion.1.after_ref), channel_id=1, source_target_pairs={{0,1},{1,0},{2,3},{3,2},{4,5},{5,4},{6,7},{7,6},{8,9},{9,8},{10,11... | collective-permute-start | bytes 350216 | tf_op jit(solution)/shard_map/ppermute | solution.py:21
  28.5 0.7 copy-start.5
  28.5 2.6 %collective-permute-start.5 = (bf16[16,7296]{1,0:T(8,128)(2,1)S(1)}, bf16[16,7296]{1,0:T(8,128)(2,1)S(1)}, u32[]{:S(2)}, u32[]{:S(2)}) collective-permute-start(bf16[16,7296]{1,0:T(8,128)(2,1)S(1)} %pad_maximum_fusion.after_ref.own_ref), channel_id=1, source_target_pairs={{0,8},{8,0},{1,9},{9,1},{2,10},{10,2},{3,11},{11,3},{4,12},{12,4},... | collective-permute-start | bytes 700424 | tf_op jit(solution)/shard_map/ppermute | solution.py:21
  31.1 0.7 copy-start.9
  53.1 1.8 %collective-permute-start.6 = (bf16[16,7168]{1,0:T(8,128)(2,1)}, bf16[16,7168]{1,0:T(8,128)(2,1)S(1)}, u32[]{:S(2)}, u32[]{:S(2)}) collective-permute-start(bf16[16,7168]{1,0:T(8,128)(2,1)} %get-tuple-element.42), channel_id=1, source_target_pairs={{0,8},{8,0},{1,9},{9,1},{2,10},{10,2},{3,11},{11,3},{4,12},{12,4},... | collective-permute-start | bytes 688136 | tf_op jit(solution)/shard_map/ppermute | solution.py:21
  55.9 5.3 %collective-permute-start.7 = (bf16[8,7168]{1,0:T(8,128)(2,1)S(1)}, bf16[8,7168]{1,0:T(8,128)(2,1)S(1)}, u32[]{:S(2)}, u32[]{:S(2)}) collective-permute-start(bf16[8,7168]{1,0:T(8,128)(2,1)S(1)} %slice.93), channel_id=1, source_target_pairs={{0,1},{1,0},{2,3},{3,2},{4,5},{5,4},{6,7},{7,6},{8,9},{9,8},{10,11... | collective-permute-start | bytes 344072 | tf_op jit(solution)/shard_map/ppermute | solution.py:21
  61.2 4.2 %collective-permute-start.8 = (bf16[4,7168]{1,0:T(4,128)(2,1)S(1)}, bf16[4,7168]{1,0:T(4,128)(2,1)S(1)}, u32[]{:S(2)}, u32[]{:S(2)}) collective-permute-start(bf16[4,7168]{1,0:T(4,128)(2,1)S(1)} %slice.94), channel_id=1, source_target_pairs={{0,2},{1,3},{2,0},{3,1},{4,6},{5,7},{6,4},{7,5},{8,10},{9,11},{10,... | collective-permute-start | bytes 172040 | tf_op jit(solution)/shard_map/ppermute | solution.py:21
  65.5 4.8 %collective-permute-start.9 = (bf16[2,7168]{1,0:T(2,128)(2,1)S(1)}, bf16[2,7168]{1,0:T(2,128)(2,1)S(1)}, u32[]{:S(2)}, u32[]{:S(2)}) collective-permute-start(bf16[2,7168]{1,0:T(2,128)(2,1)S(1)} %slice.96), channel_id=1, source_target_pairs={{0,4},{1,5},{2,6},{3,7},{4,0},{5,1},{6,2},{7,3},{8,12},{9,13},{10,... | collective-permute-start | bytes 86024 | tf_op jit(solution)/shard_map/ppermute | solution.py:21

commit v4 on v3

--- a/solution.py
+++ b/solution.py
@@ -168,7 +168,7 @@
     slots = SLOTS
     return pl.pallas_call(
         functools.partial(expert_kernel, lax.axis_size("local"), chunk),
-        out_shape=(jax.ShapeDtypeStruct((half, depth), BF16), jax.ShapeDtypeStruct((half, depth), BF16)),
+        out_shape=(jax.ShapeDtypeStruct((half, depth), BF16), pltpu.VMEM((half, depth), BF16)),
         in_specs=[VMEM, VMEM, VMEM, ANYWHERE, ANYWHERE],
         out_specs=(VMEM, VMEM),
         scratch_shapes=[

time: 71.3 us -> 92.7 us (1.30)
  local copies, waits for them, and re-layouts: 1.86 us -> 23.5 us
    unnamed x26 -> x30, local copies, waits for them, and re-layouts: 1.72 us -> 23.3 us
  transfers between devices with their start and end apart: 10 -> 10, of which waited for: 7 -> 7; matrix products, arithmetic and copies ran while one was open for 0% -> 0% of each run, Pallas kernels for 21% -> 16%
where the time goes in v4:
time: 92.7 us; the launch traced here: 92.3 us
  Pallas kernels  38.4 us (41%)
  local copies, waits for them, and re-layouts  23.5 us (25%)
  starting transfers between devices  17.1 us (18%)
  waiting for transfers between devices  10.6 us (11%)
  other arithmetic  2.42 us (3%)
    unnamed x30, local copies, waits for them, and re-layouts  23.3 us
    pallas_call x1, Pallas kernels, expert(): pl.pallas_call(functools.partial(expert_kernel, lax.axis_size('local'), c...  21.2 us
    ppermute x10, starting transfers between devices, swap(): lax.ppermute(x, axis, [(i, i ^ bit) for i in range(lax.axis_size(axis))])  17.1 us
    pallas_call x7, Pallas kernels, fetch(): pl.pallas_call(functools.partial(fetch_kernel, depth, first, last), out_s...  16.7 us
    ppermute x10, waiting for transfers between devices, swap(): lax.ppermute(x, axis, [(i, i ^ bit) for i in range(lax.axis_size(axis))])  10.6 us
  transfers between devices with their start and end apart: 10, of which 7 were waited for; matrix products, arithmetic and copies ran while one was open for 0% of the time, Pallas kernels for 16%

profile of v4, /device:TPU:0, one launch (start us, length us, event | category | flops | bytes accessed | tf_op | source)
XLA Modules:
  0.0 92.3 jit_solution(795802809330442992)
XLA Ops:
  0.0 1.7 %shard_map.91.refs_0_ = bf16[8192,2048]{1,0:T(8,128)(2,1)S(1)} custom-call(bf16[1,7168,2048]{2,1,0:T(8,128)(2,1)} %gate_hbm.13, bf16[1,7168,2048]{2,1,0:T(8,128)(2,1)} %up_hbm.15, bf16[16,128]{1,0:T(8,128)(2,1)} %attn_ref), custom_call_target="tpu_custom_call" | custom-call | bytes 2097152 | tf_op jit(solution)/shard_map/pallas_call | solution.py:87
  1.8 0.4 copy-done.2
  2.2 0.5 shard_map.92
  2.6 3.0 %collective-permute-start = (bf16[8,7168]{1,0:T(8,128)(2,1)S(1)}, bf16[8,7168]{1,0:T(8,128)(2,1)S(1)}, u32[]{:S(2)}, u32[]{:S(2)}) collective-permute-start(bf16[8,7168]{1,0:T(8,128)(2,1)S(1)} %get-tuple-element.26.after_ref), channel_id=1, source_target_pairs={{0,1},{1,0},{2,3},{3,2},{4,5},{5,4},{6,7},{7,6},{8,9},{9,8},{10,11... | collective-permute-start | bytes 344072 | tf_op jit(solution)/shard_map/ppermute | solution.py:21
  5.7 3.1 %shard_map.93.refs_0_ = bf16[8192,2048]{1,0:T(8,128)(2,1)S(1)} custom-call(bf16[1,7168,2048]{2,1,0:T(8,128)(2,1)} %gate_hbm.13, bf16[1,7168,2048]{2,1,0:T(8,128)(2,1)} %up_hbm.15, bf16[8,7168]{1,0:T(8,128)(2,1)} %copy-done.3, bf16[8192,2048]{1,0:T(8,128)(2,1)S(1)} %shard_map.91.refs_0_), custom_call_target="tpu_custom_call", output_to_operand_aliasing={{}: (3, {})} | custom-call | bytes 7340032 | tf_op jit(solution)/shard_map/pallas_call | solution.py:87
  8.9 1.9 %collective-permute-start.1 = (bf16[4,7168]{1,0:T(4,128)(2,1)S(1)}, bf16[4,7168]{1,0:T(4,128)(2,1)S(1)}, u32[]{:S(2)}, u32[]{:S(2)}) collective-permute-start(bf16[4,7168]{1,0:T(4,128)(2,1)S(1)} %slice.95.after_ref), channel_id=1, source_target_pairs={{0,2},{1,3},{2,0},{3,1},{4,6},{5,7},{6,4},{7,5},{8,10},{9,11},{10,... | collective-permute-start | bytes 172040 | tf_op jit(solution)/shard_map/ppermute | solution.py:21
  10.8 2.2 %shard_map.94.refs_0_ = bf16[8192,2048]{1,0:T(8,128)(2,1)S(1)} custom-call(bf16[1,7168,2048]{2,1,0:T(8,128)(2,1)} %gate_hbm.13, bf16[1,7168,2048]{2,1,0:T(8,128)(2,1)} %up_hbm.15, bf16[4,7168]{1,0:T(4,128)(2,1)} %copy-done.12, bf16[8192,2048]{1,0:T(8,128)(2,1)S(1)} %shard_map.93.refs_0_), custom_call_target="tpu_custom_call", output_to_operand_aliasing={{}: (3, {})} | custom-call | bytes 4194304 | tf_op jit(solution)/shard_map/pallas_call | solution.py:87
  13.0 0.2 collective-permute-done.1
  13.3 2.9 %collective-permute-start.2 = (bf16[4,7296]{1,0:T(4,128)(2,1)S(1)}, bf16[4,7296]{1,0:T(4,128)(2,1)S(1)}, u32[]{:S(2)}, u32[]{:S(2)}) collective-permute-start(bf16[4,7296]{1,0:T(4,128)(2,1)S(1)} %fusion.3.after_ref), channel_id=1, source_target_pairs={{0,4},{1,5},{2,6},{3,7},{4,0},{5,1},{6,2},{7,3},{8,12},{9,13},{10,... | collective-permute-start | bytes 175112 | tf_op jit(solution)/shard_map/ppermute | solution.py:21
  16.2 2.5 %shard_map.95.refs_0_ = bf16[8192,2048]{1,0:T(8,128)(2,1)S(1)} custom-call(bf16[1,7168,2048]{2,1,0:T(8,128)(2,1)} %gate_hbm.13, bf16[1,7168,2048]{2,1,0:T(8,128)(2,1)} %up_hbm.15, bf16[4,7296]{1,0:T(4,128)(2,1)} %copy-done.9, bf16[8192,2048]{1,0:T(8,128)(2,1)S(1)} %shard_map.94.refs_0_), custom_call_target="tpu_custom_call", output_to_operand_aliasing={{}: (3, {})} | custom-call | bytes 5242880 | tf_op jit(solution)/shard_map/pallas_call | solution.py:87
  18.8 0.2 multiply_reduce_fusion
  19.2 1.6 %collective-permute-start.3 = (bf16[4,7296]{1,0:T(4,128)(2,1)S(1)}, bf16[4,7296]{1,0:T(4,128)(2,1)S(1)}, u32[]{:S(2)}, u32[]{:S(2)}) collective-permute-start(bf16[4,7296]{1,0:T(4,128)(2,1)S(1)} %maximum_maximum_fusion.after_ref), channel_id=1, source_target_pairs={{0,2},{1,3},{2,0},{3,1},{4,6},{5,7},{6,4},{7,5},{8,10},{9,11},{10,... | collective-permute-start | bytes 175112 | tf_op jit(solution)/shard_map/ppermute | solution.py:21
  20.8 2.2 %shard_map.96.refs_0_ = bf16[8192,2048]{1,0:T(8,128)(2,1)S(1)} custom-call(bf16[1,7168,2048]{2,1,0:T(8,128)(2,1)} %gate_hbm.13, bf16[1,7168,2048]{2,1,0:T(8,128)(2,1)} %up_hbm.15, bf16[4,7296]{1,0:T(4,128)(2,1)} %copy-done.10, bf16[8192,2048]{1,0:T(8,128)(2,1)S(1)} %shard_map.95.refs_0_), custom_call_target="tpu_custom_call", output_to_operand_aliasing={{}: (3, {})} | custom-call | bytes 4194304 | tf_op jit(solution)/shard_map/pallas_call | solution.py:87
  23.1 0.4 collective-permute-done.3
  23.5 1.6 %collective-permute-start.4 = (bf16[8,7296]{1,0:T(8,128)(2,1)S(1)}, bf16[8,7296]{1,0:T(8,128)(2,1)S(1)}, u32[]{:S(2)}, u32[]{:S(2)}) collective-permute-start(bf16[8,7296]{1,0:T(8,128)(2,1)S(1)} %pad_maximum_fusion.1.after_ref), channel_id=1, source_target_pairs={{0,1},{1,0},{2,3},{3,2},{4,5},{5,4},{6,7},{7,6},{8,9},{9,8},{10,11... | collective-permute-start | bytes 350216 | tf_op jit(solution)/shard_map/ppermute | solution.py:21
  25.1 3.1 %shard_map.97.refs_0_ = bf16[8192,2048]{1,0:T(8,128)(2,1)S(1)} custom-call(bf16[1,7168,2048]{2,1,0:T(8,128)(2,1)} %gate_hbm.13, bf16[1,7168,2048]{2,1,0:T(8,128)(2,1)} %up_hbm.15, bf16[8,7296]{1,0:T(8,128)(2,1)} %copy-done.8, bf16[8192,2048]{1,0:T(8,128)(2,1)S(1)} %shard_map.96.refs_0_), custom_call_target="tpu_custom_call", output_to_operand_aliasing={{}: (3, {})} | custom-call | bytes 7340032 | tf_op jit(solution)/shard_map/pallas_call | solution.py:87
  28.2 0.2 collective-permute-done.4
  28.6 0.6 copy-done.7
  29.2 1.9 %shard_map.98.held_ref = bf16[8192,2048]{1,0:T(8,128)(2,1)S(1)} custom-call(bf16[1,7168,2048]{2,1,0:T(8,128)(2,1)} %gate_hbm.13, bf16[1,7168,2048]{2,1,0:T(8,128)(2,1)} %up_hbm.15, bf16[16,7296]{1,0:T(8,128)(2,1)} %copy-done.7, bf16[8192,2048]{1,0:T(8,128)(2,1)S(1)} %shard_map.97.refs_0_), custom_call_target="tpu_custom_call", output_to_operand_aliasing={{}: (3, {})} | custom-call | bytes 3145728 | tf_op jit(solution)/shard_map/pallas_call | solution.py:87
  31.1 11.1 %copy-done = bf16[8192,2048]{1,0:T(8,128)(2,1)} copy-done((bf16[8192,2048]{1,0:T(8,128)(2,1)}, bf16[8192,2048]{1,0:T(8,128)(2,1)S(1)}, u32[]{:S(2)}) %copy-start) | copy-done | bytes 33554456
  42.2 0.7 copy-done.11
  42.9 10.5 %copy-done.1 = bf16[8192,2048]{1,0:T(8,128)(2,1)S(1)} copy-done((bf16[8192,2048]{1,0:T(8,128)(2,1)S(1)}, bf16[8192,2048]{1,0:T(8,128)(2,1)}, u32[]{:S(2)}) %copy-start.1) | copy-done | bytes 33554456
  53.4 21.2 %shard_map.99 = (bf16[16,7168]{1,0:T(8,128)(2,1)}, bf16[16,7168]{1,0:T(8,128)(2,1)S(1)}) custom-call(bf16[16,7296]{1,0:T(8,128)(2,1)} %copy-done.7, bf16[16,7296]{1,0:T(8,128)(2,1)} %copy-done.11, bf16[8192,2048]{1,0:T(8,128)(2,1)S(1)} %copy-done.1, bf16[1,7168,2048]{2,1,0:T(8,128)(2,1)} %up_hbm.15, bf16[1,2048,7168]{2,1,0:T(8,128)(2,1)} %down_hbm.1), custom_call_target="tpu_custom_call" | custom-call | flops 2818572288 | bytes 58720256 | tf_op jit(solution)/shard_map/pallas_call | solution.py:169
  74.7 1.5 %collective-permute-done.6 = bf16[16,7168]{1,0:T(8,128)(2,1)S(1)} collective-permute-done((bf16[16,7168]{1,0:T(8,128)(2,1)S(1)}, bf16[16,7168]{1,0:T(8,128)(2,1)S(1)}, u32[]{:S(2)}, u32[]{:S(2)}) %collective-permute-start.6) | collective-permute-done | bytes 229408 | tf_op jit(solution)/shard_map/ppermute | solution.py:21
  76.2 1.0 %convert_add_fusion = f32[16,7168]{1,0:T(8,128)S(1)} fusion(bf16[16,7168]{1,0:T(8,128)(2,1)S(1)} %collective-permute-done.6, bf16[16,7168]{1,0:T(8,128)(2,1)} %get-tuple-element.41), kind=kLoop, calls=%fused_computation | loop fusion | flops 344064 | bytes 917504 | tf_op jit(solution)/shard_map/add | solution.py:234
  77.2 1.6 %collective-permute-start.7 = (bf16[8,7168]{1,0:T(8,128)(2,1)S(1)}, bf16[8,7168]{1,0:T(8,128)(2,1)S(1)}, u32[]{:S(2)}, u32[]{:S(2)}) collective-permute-start(bf16[8,7168]{1,0:T(8,128)(2,1)S(1)} %slice.93), channel_id=1, source_target_pairs={{0,1},{1,0},{2,3},{3,2},{4,5},{5,4},{6,7},{7,6},{8,9},{9,8},{10,11... | collective-permute-start | bytes 344072 | tf_op jit(solution)/shard_map/ppermute | solution.py:21
  78.8 3.7 %collective-permute-done.7 = bf16[8,7168]{1,0:T(8,128)(2,1)S(1)} collective-permute-done((bf16[8,7168]{1,0:T(8,128)(2,1)S(1)}, bf16[8,7168]{1,0:T(8,128)(2,1)S(1)}, u32[]{:S(2)}, u32[]{:S(2)}) %collective-permute-start.7) | collective-permute-done | bytes 114720 | tf_op jit(solution)/shard_map/ppermute | solution.py:21
  82.5 1.6 %collective-permute-start.8 = (bf16[4,7168]{1,0:T(4,128)(2,1)S(1)}, bf16[4,7168]{1,0:T(4,128)(2,1)S(1)}, u32[]{:S(2)}, u32[]{:S(2)}) collective-permute-start(bf16[4,7168]{1,0:T(4,128)(2,1)S(1)} %slice.94), channel_id=1, source_target_pairs={{0,2},{1,3},{2,0},{3,1},{4,6},{5,7},{6,4},{7,5},{8,10},{9,11},{10,... | collective-permute-start | bytes 172040 | tf_op jit(solution)/shard_map/ppermute | solution.py:21
  84.2 2.6 %collective-permute-done.8 = bf16[4,7168]{1,0:T(4,128)(2,1)S(1)} collective-permute-done((bf16[4,7168]{1,0:T(4,128)(2,1)S(1)}, bf16[4,7168]{1,0:T(4,128)(2,1)S(1)}, u32[]{:S(2)}, u32[]{:S(2)}) %collective-permute-start.8) | collective-permute-done | bytes 57376 | tf_op jit(solution)/shard_map/ppermute | solution.py:21
  86.8 2.7 %collective-permute-start.9 = (bf16[2,7168]{1,0:T(2,128)(2,1)S(1)}, bf16[2,7168]{1,0:T(2,128)(2,1)S(1)}, u32[]{:S(2)}, u32[]{:S(2)}) collective-permute-start(bf16[2,7168]{1,0:T(2,128)(2,1)S(1)} %slice.96), channel_id=1, source_target_pairs={{0,4},{1,5},{2,6},{3,7},{4,0},{5,1},{6,2},{7,3},{8,12},{9,13},{10,... | collective-permute-start | bytes 86024 | tf_op jit(solution)/shard_map/ppermute | solution.py:21
  89.6 2.1 %collective-permute-done.9 = bf16[2,7168]{1,0:T(2,128)(2,1)S(1)} collective-permute-done((bf16[2,7168]{1,0:T(2,128)(2,1)S(1)}, bf16[2,7168]{1,0:T(2,128)(2,1)S(1)}, u32[]{:S(2)}, u32[]{:S(2)}) %collective-permute-start.9) | collective-permute-done | bytes 28704 | tf_op jit(solution)/shard_map/ppermute | solution.py:21
  91.7 0.7 fusion.5
  (49 shorter events, 0.9 us)
Async XLA Ops:
  0.0 1.8 %copy-start.4 = (bf16[16,128]{1,0:T(8,128)(2,1)S(1)}, bf16[16,128]{1,0:T(8,128)(2,1)}, u32[]{:S(2)}) copy-start(bf16[16,128]{1,0:T(8,128)(2,1)} %attn_ref) | copy-start | bytes 12292
  0.0 1.8 %copy-start.6 = (bf16[2,8]{1,0:T(2,128)(2,1)S(1)}, bf16[2,8]{1,0:T(2,128)(2,1)}, u32[]{:S(2)}) copy-start(bf16[2,8]{1,0:T(2,128)(2,1)} %route_w_ref.1) | copy-start | bytes 100
  0.0 1.8 %copy-start.5 = (s32[2,8]{1,0:T(2,128)S(1)}, s32[2,8]{1,0:T(2,128)}, u32[]{:S(2)}) copy-start(s32[2,8]{1,0:T(2,128)} %routes_ref.1) | copy-start | bytes 196
  0.0 2.2 %copy-start.2 = (bf16[128,7168]{1,0:T(8,128)(2,1)S(1)}, bf16[128,7168]{1,0:T(8,128)(2,1)}, u32[]{:S(2)}) copy-start(bf16[128,7168]{1,0:T(8,128)(2,1)} %proj_ref.1) | copy-start | bytes 5505028
  2.6 3.0 %copy-start.3 = (bf16[8,7168]{1,0:T(8,128)(2,1)}, bf16[8,7168]{1,0:T(8,128)(2,1)S(1)}, u32[]{:S(2)}) copy-start(bf16[8,7168]{1,0:T(8,128)(2,1)S(1)} %get-tuple-element.26.after_ref) | copy-start | bytes 344068
  2.6 6.2 %collective-permute-start = (bf16[8,7168]{1,0:T(8,128)(2,1)S(1)}, bf16[8,7168]{1,0:T(8,128)(2,1)S(1)}, u32[]{:S(2)}, u32[]{:S(2)}) collective-permute-start(bf16[8,7168]{1,0:T(8,128)(2,1)S(1)} %get-tuple-element.26.after_ref), channel_id=1, source_target_pairs={{0,1},{1,0},{2,3},{3,2},{4,5},{5,4},{6,7},{7,6},{8,9},{9,8},{10,11... | collective-permute-start | bytes 344072 | tf_op jit(solution)/shard_map/ppermute | solution.py:21
  8.9 1.9 %copy-start.12 = (bf16[4,7168]{1,0:T(4,128)(2,1)}, bf16[4,7168]{1,0:T(4,128)(2,1)S(1)}, u32[]{:S(2)}) copy-start(bf16[4,7168]{1,0:T(4,128)(2,1)S(1)} %slice.95.after_ref) | copy-start | bytes 172036
  8.9 4.2 %collective-permute-start.1 = (bf16[4,7168]{1,0:T(4,128)(2,1)S(1)}, bf16[4,7168]{1,0:T(4,128)(2,1)S(1)}, u32[]{:S(2)}, u32[]{:S(2)}) collective-permute-start(bf16[4,7168]{1,0:T(4,128)(2,1)S(1)} %slice.95.after_ref), channel_id=1, source_target_pairs={{0,2},{1,3},{2,0},{3,1},{4,6},{5,7},{6,4},{7,5},{8,10},{9,11},{10,... | collective-permute-start | bytes 172040 | tf_op jit(solution)/shard_map/ppermute | solution.py:21
  10.7 2.4 %copy-start.14 = (bf16[2,7168]{1,0:T(2,128)(2,1)S(1)}, bf16[2,7168]{1,0:T(2,128)(2,1)}, u32[]{:S(2)}) copy-start(bf16[2,7168]{1,0:T(2,128)(2,1)} %param.11) | copy-start | bytes 86020
  13.3 2.9 %copy-start.9 = (bf16[4,7296]{1,0:T(4,128)(2,1)}, bf16[4,7296]{1,0:T(4,128)(2,1)S(1)}, u32[]{:S(2)}) copy-start(bf16[4,7296]{1,0:T(4,128)(2,1)S(1)} %fusion.3.after_ref) | copy-start | bytes 175108
  13.3 5.7 %copy-start.13 = (f32[7168]{0:T(1024)S(1)}, f32[7168]{0:T(1024)}, u32[]{:S(2)}) copy-start(f32[7168]{0:T(1024)} %param.12) | copy-start | bytes 86020
  13.3 5.4 %collective-permute-start.2 = (bf16[4,7296]{1,0:T(4,128)(2,1)S(1)}, bf16[4,7296]{1,0:T(4,128)(2,1)S(1)}, u32[]{:S(2)}, u32[]{:S(2)}) collective-permute-start(bf16[4,7296]{1,0:T(4,128)(2,1)S(1)} %fusion.3.after_ref), channel_id=1, source_target_pairs={{0,4},{1,5},{2,6},{3,7},{4,0},{5,1},{6,2},{7,3},{8,12},{9,13},{10,... | collective-permute-start | bytes 175112 | tf_op jit(solution)/shard_map/ppermute | solution.py:21
  19.2 1.7 %copy-start.10 = (bf16[4,7296]{1,0:T(4,128)(2,1)}, bf16[4,7296]{1,0:T(4,128)(2,1)S(1)}, u32[]{:S(2)}) copy-start(bf16[4,7296]{1,0:T(4,128)(2,1)S(1)} %maximum_maximum_fusion.after_ref) | copy-start | bytes 175108
  19.2 4.3 %collective-permute-start.3 = (bf16[4,7296]{1,0:T(4,128)(2,1)S(1)}, bf16[4,7296]{1,0:T(4,128)(2,1)S(1)}, u32[]{:S(2)}, u32[]{:S(2)}) collective-permute-start(bf16[4,7296]{1,0:T(4,128)(2,1)S(1)} %maximum_maximum_fusion.after_ref), channel_id=1, source_target_pairs={{0,2},{1,3},{2,0},{3,1},{4,6},{5,7},{6,4},{7,5},{8,10},{9,11},{10,... | collective-permute-start | bytes 175112 | tf_op jit(solution)/shard_map/ppermute | solution.py:21
  23.5 1.6 %copy-start.8 = (bf16[8,7296]{1,0:T(8,128)(2,1)}, bf16[8,7296]{1,0:T(8,128)(2,1)S(1)}, u32[]{:S(2)}) copy-start(bf16[8,7296]{1,0:T(8,128)(2,1)S(1)} %pad_maximum_fusion.1.after_ref) | copy-start | bytes 350212
  23.5 4.9 %collective-permute-start.4 = (bf16[8,7296]{1,0:T(8,128)(2,1)S(1)}, bf16[8,7296]{1,0:T(8,128)(2,1)S(1)}, u32[]{:S(2)}, u32[]{:S(2)}) collective-permute-start(bf16[8,7296]{1,0:T(8,128)(2,1)S(1)} %pad_maximum_fusion.1.after_ref), channel_id=1, source_target_pairs={{0,1},{1,0},{2,3},{3,2},{4,5},{5,4},{6,7},{7,6},{8,9},{9,8},{10,11... | collective-permute-start | bytes 350216 | tf_op jit(solution)/shard_map/ppermute | solution.py:21
  28.5 0.7 copy-start.7
  28.5 13.7 %collective-permute-start.5 = (bf16[16,7296]{1,0:T(8,128)(2,1)S(1)}, bf16[16,7296]{1,0:T(8,128)(2,1)S(1)}, u32[]{:S(2)}, u32[]{:S(2)}) collective-permute-start(bf16[16,7296]{1,0:T(8,128)(2,1)S(1)} %pad_maximum_fusion.after_ref.own_ref), channel_id=1, source_target_pairs={{0,8},{8,0},{1,9},{9,1},{2,10},{10,2},{3,11},{11,3},{4,12},{12,4},... | collective-permute-start | bytes 700424 | tf_op jit(solution)/shard_map/ppermute | solution.py:21
  31.1 11.1 %copy-start = (bf16[8192,2048]{1,0:T(8,128)(2,1)}, bf16[8192,2048]{1,0:T(8,128)(2,1)S(1)}, u32[]{:S(2)}) copy-start(bf16[8192,2048]{1,0:T(8,128)(2,1)S(1)} %shard_map.98.held_ref) | copy-start | bytes 100663296
  42.2 0.7 copy-start.11
  42.9 10.5 %copy-start.1 = (bf16[8192,2048]{1,0:T(8,128)(2,1)S(1)}, bf16[8192,2048]{1,0:T(8,128)(2,1)}, u32[]{:S(2)}) copy-start(bf16[8192,2048]{1,0:T(8,128)(2,1)} %copy-done) | copy-start | bytes 100663296
  74.6 1.6 %collective-permute-start.6 = (bf16[16,7168]{1,0:T(8,128)(2,1)S(1)}, bf16[16,7168]{1,0:T(8,128)(2,1)S(1)}, u32[]{:S(2)}, u32[]{:S(2)}) collective-permute-start(bf16[16,7168]{1,0:T(8,128)(2,1)S(1)} %get-tuple-element.42), channel_id=1, source_target_pairs={{0,8},{8,0},{1,9},{9,1},{2,10},{10,2},{3,11},{11,3},{4,12},{12,4},... | collective-permute-start | bytes 688136 | tf_op jit(solution)/shard_map/ppermute | solution.py:21
  77.2 5.3 %collective-permute-start.7 = (bf16[8,7168]{1,0:T(8,128)(2,1)S(1)}, bf16[8,7168]{1,0:T(8,128)(2,1)S(1)}, u32[]{:S(2)}, u32[]{:S(2)}) collective-permute-start(bf16[8,7168]{1,0:T(8,128)(2,1)S(1)} %slice.93), channel_id=1, source_target_pairs={{0,1},{1,0},{2,3},{3,2},{4,5},{5,4},{6,7},{7,6},{8,9},{9,8},{10,11... | collective-permute-start | bytes 344072 | tf_op jit(solution)/shard_map/ppermute | solution.py:21
  82.5 4.2 %collective-permute-start.8 = (bf16[4,7168]{1,0:T(4,128)(2,1)S(1)}, bf16[4,7168]{1,0:T(4,128)(2,1)S(1)}, u32[]{:S(2)}, u32[]{:S(2)}) collective-permute-start(bf16[4,7168]{1,0:T(4,128)(2,1)S(1)} %slice.94), channel_id=1, source_target_pairs={{0,2},{1,3},{2,0},{3,1},{4,6},{5,7},{6,4},{7,5},{8,10},{9,11},{10,... | collective-permute-start | bytes 172040 | tf_op jit(solution)/shard_map/ppermute | solution.py:21
  86.8 4.8 %collective-permute-start.9 = (bf16[2,7168]{1,0:T(2,128)(2,1)S(1)}, bf16[2,7168]{1,0:T(2,128)(2,1)S(1)}, u32[]{:S(2)}, u32[]{:S(2)}) collective-permute-start(bf16[2,7168]{1,0:T(2,128)(2,1)S(1)} %slice.96), channel_id=1, source_target_pairs={{0,4},{1,5},{2,6},{3,7},{4,0},{5,1},{6,2},{7,3},{8,12},{9,13},{10,... | collective-permute-start | bytes 86024 | tf_op jit(solution)/shard_map/ppermute | solution.py:21
